TPU v7x, 32 devices: a whole 2x2x4 slice. The times are simulated.
32 devices in a mesh: grp: 2 (over y), slab: 4 (over z), coil: 2 (over x), half: 2 (over core).
Axes of the slice: x: 2, y: 2, z: 4, core: 2. Of those that a mesh axis runs over, the one named last changes fastest.
Arguments:
- kspace: bfloat16 [32, 4, 128, 640], P(('grp', 'coil', 'half'), None, 'slab'), parts along dimension 0, may hold values from -6 to 6
- measured: bfloat16 [32, 4, 128, 640], P(('grp', 'coil', 'half'), None, 'slab'), parts along dimension 0, may hold values from -6 to 6
- cotangent: bfloat16 [32, 4, 128, 640], P(('grp', 'coil', 'half'), None, 'slab'), parts along dimension 0, may hold values from -0.014770508 to 0.014770508
- coil_maps: bfloat16 [32, 4, 128, 640], P(('grp', 'coil', 'half'), 'slab'), parts along dimension 0, may hold values from -3 to 3
- sample_mask: int32 [256, 320], P(('grp', 'slab')), parts along dimension 0, may hold values 0 or 1
- step_size: float32 [1], replicated, may hold values from 0.5 to 1.5
- weight_first: bfloat16 [3, 3, 32, 3, 2], replicated, may hold values from -0.875 to 0.875
- weight_middle: bfloat16 [3, 3, 32, 3, 32], replicated, may hold values from -0.21875 to 0.21875
- weight_last: bfloat16 [3, 3, 2, 3, 32], replicated, may hold values from -0.21875 to 0.21875
Outputs:
- updated: bfloat16 [32, 4, 128, 640], P(('grp', 'coil', 'half'), None, 'slab'), parts along dimension 0
- grad_first: float32 [6, 3, 32, 3, 2], P('grp'), parts along dimension 0
- grad_middle: float32 [6, 3, 32, 3, 32], P('grp'), parts along dimension 0
- grad_last: float32 [6, 3, 2, 3, 32], P('grp'), parts along dimension 0
There are 2 independent parts, one for each index of `grp`. A program takes and returns all parts, laid end to end along the dimension named above; an argument that names none is the same for every part. Nothing has to cross between parts.
Inputs may be any that keep to these rules, and one draw needn't show every extreme that they name: `sample_mask`: 1 where the phase-encode line (kz, ky) was acquired.
All inputs are finite; a program needn't handle non-finite values. No bound on the sum of `sample_mask` on one device may be relied on, other than what follows from the above.
Results may differ from a plain program's by a relative error of at most 0.0091.
Values may be sent and summed in bfloat16 or wider, within the bound.
A program may use at most 64 MiB of HBM per device.

v0:
```python
import functools
import math

import jax
import jax.numpy as jnp
import ml_dtypes
import numpy as np
from jax import lax
from jax.experimental import pallas as pl
from jax.experimental.pallas import tpu as pltpu
from jax.sharding import PartitionSpec as P


def with_halo(block, sides, width):
    for axis, dim in sides:
        count = lax.axis_size(axis)
        forward = [(i, i + 1) for i in range(count - 1)]
        backward = [(target, source) for source, target in forward]
        low = lax.ppermute(
            lax.slice_in_dim(block, block.shape[dim] - width, None, axis=dim), axis, forward
        )
        high = lax.ppermute(lax.slice_in_dim(block, 0, width, axis=dim), axis, backward)
        block = jnp.concatenate([low, block, high], axis=dim)
    return block


def dft_parts(length):
    position = lax.iota(jnp.int32, length)
    product = position[:, None] * position[None, :] % length
    angles = product.astype(jnp.float32) * (2.0 * math.pi / length)
    factor = 1.0 / math.sqrt(length)
    return (jnp.cos(angles) * factor, jnp.sin(angles) * factor)


def plane_table(length, orient):
    cos_part, sin_part = dft_parts(length)
    upper_rows = jnp.concatenate([cos_part, orient * sin_part], axis=1)
    lower_rows = jnp.concatenate([-orient * sin_part, cos_part], axis=1)
    return jnp.concatenate([upper_rows, lower_rows], axis=0)


def along_y(values, table):
    return jnp.einsum(
        "cxzk,kw->cxzw",
        values,
        table,
        precision=lax.Precision.HIGH,
        preferred_element_type=jnp.float32,
    )


def along_z(values, orient):
    length = values.shape[2]
    half_len = values.shape[3] // 2
    cos_part, sin_part = dft_parts(length)
    stacked = jnp.concatenate([cos_part, sin_part], axis=0)
    mixture = jnp.einsum(
        "wz,cxzk->cxwk",
        stacked,
        values,
        precision=lax.Precision.HIGH,
        preferred_element_type=jnp.float32,
    )
    direct = mixture[:, :, :length]
    crossed = mixture[:, :, length:]
    turned = jnp.concatenate(
        [-orient * crossed[..., half_len:], orient * crossed[..., :half_len]], axis=-1
    )
    return direct + turned


def coil_adjoint(lines, coil_maps):
    half_len = lines.shape[3] // 2
    map_values = coil_maps.astype(jnp.float32)
    map_real = map_values[..., :half_len]
    map_imag = map_values[..., half_len:]
    line_real = lines[..., :half_len]
    line_imag = lines[..., half_len:]
    real_sum = jnp.sum(map_real * line_real + map_imag * line_imag, axis=0)
    imag_sum = jnp.sum(map_real * line_imag - map_imag * line_real, axis=0)
    return jnp.stack([real_sum, imag_sum], axis=2)


def coil_expand(image, coil_maps):
    half_len = coil_maps.shape[3] // 2
    map_values = coil_maps.astype(jnp.float32)
    map_real = map_values[..., :half_len]
    map_imag = map_values[..., half_len:]
    image_real = image[:, :, 0].astype(jnp.float32)
    image_imag = image[:, :, 1].astype(jnp.float32)
    out_real = map_real * image_real - map_imag * image_imag
    out_imag = map_real * image_imag + map_imag * image_real
    return jnp.concatenate([out_real, out_imag], axis=-1)


def with_rims(values):
    return with_halo(values, (("slab", 0), (("coil", "half"), 1)), 1)


def columns_of(padded):
    y_count = padded.shape[3]
    widened = jnp.pad(padded, ((0, 0), (0, 0), (0, 0), (1, 1)))
    return jnp.concatenate(
        [widened[..., shift_y : shift_y + y_count] for shift_y in range(3)], axis=2
    )


def conv_apply(columns, matrix):
    x_count = columns.shape[0] - 2
    z_count = columns.shape[1] - 2
    summed = None
    for shift_x in range(3):
        for shift_z in range(3):
            partial_sum = jnp.einsum(
                "ok,xzky->xzoy",
                matrix[shift_x, shift_z],
                columns[shift_x : shift_x + x_count, shift_z : shift_z + z_count],
                preferred_element_type=jnp.float32,
            )
            summed = partial_sum if summed is None else summed + partial_sum
    return summed


def weight_grad(out_grad, columns):
    x_count = out_grad.shape[0]
    z_count = out_grad.shape[1]
    outer_list = []
    for shift_x in range(3):
        inner_list = []
        for shift_z in range(3):
            inner_list.append(
                jnp.einsum(
                    "xzoy,xzky->ok",
                    out_grad,
                    columns[shift_x : shift_x + x_count, shift_z : shift_z + z_count],
                    preferred_element_type=jnp.float32,
                )
            )
        outer_list.append(jnp.stack(inner_list, axis=0))
    return jnp.stack(outer_list, axis=0)


def as_matrix(weight):
    return weight.reshape(3, 3, weight.shape[2], 3 * weight.shape[4])


def flipped(weight):
    turned = jnp.transpose(jnp.flip(weight, (0, 1, 3)), (0, 1, 4, 3, 2))
    return turned.reshape(3, 3, weight.shape[4], 3 * weight.shape[2])


def silu_grad(values):
    sigma = jax.nn.sigmoid(values)
    return sigma * (1.0 + values * (1.0 - sigma))


def shards_small_chunks(
    kspace,
    measured,
    cotangent,
    coil_maps,
    sample_mask,
    step_size,
    weight_first,
    weight_middle,
    weight_last,
):
    half_len = kspace.shape[3] // 2
    inverse_y = plane_table(half_len, 1.0)
    k_moved, g_moved = (
        lax.all_to_all(kspace, "slab", split_axis=1, concat_axis=2, tiled=True),
        lax.all_to_all(cotangent, "slab", split_axis=1, concat_axis=2, tiled=True),
    )
    k_lines = along_y(k_moved.astype(jnp.float32), inverse_y)
    g_lines = along_y(g_moved.astype(jnp.float32), inverse_y)
    image_full = coil_adjoint(along_z(k_lines, 1.0), coil_maps)
    adjoint_full = coil_adjoint(along_z(g_lines, 1.0), coil_maps)
    summed_image, summed_adjoint = lax.psum((image_full, adjoint_full), ("coil", "half"))
    z_count = summed_image.shape[1] // lax.axis_size(("coil", "half"))
    start = lax.axis_index(("coil", "half")) * z_count
    image = lax.dynamic_slice_in_dim(summed_image, start, z_count, 1)
    adjoint = lax.dynamic_slice_in_dim(summed_adjoint, start, z_count, 1)
    layer_zero = image.astype(jnp.bfloat16)
    cols_zero = columns_of(with_rims(layer_zero))
    pre_first = conv_apply(cols_zero, as_matrix(weight_first))
    act_first = jax.nn.silu(pre_first).astype(jnp.bfloat16)
    cols_first = columns_of(with_rims(act_first))
    pre_middle = conv_apply(cols_first, as_matrix(weight_middle))
    act_middle = jax.nn.silu(pre_middle).astype(jnp.bfloat16)
    cols_middle = columns_of(with_rims(act_middle))
    refined = conv_apply(cols_middle, as_matrix(weight_last)).astype(jnp.bfloat16)
    refined_all = lax.all_gather(refined, ("coil", "half"), axis=1, tiled=True)
    spectra_lines = along_z(coil_expand(refined_all, coil_maps), -1.0)
    spectra_slab = lax.all_to_all(
        spectra_lines.astype(jnp.bfloat16), "slab", split_axis=2, concat_axis=1, tiled=True
    ).astype(spectra_lines.dtype)
    model_term = along_y(spectra_slab, plane_table(half_len, -1.0))
    sampled = sample_mask.astype(jnp.float32)
    sampled = jnp.concatenate([sampled, sampled], axis=1)
    current = kspace.astype(jnp.float32)
    updated = (
        current - step_size[0] * sampled * (current - measured.astype(jnp.float32)) - model_term
    ).astype(jnp.bfloat16)
    grad_out = (-adjoint).astype(jnp.bfloat16)
    grad_last = weight_grad(grad_out, cols_middle)
    back_middle = conv_apply(columns_of(with_rims(grad_out)), flipped(weight_last))
    grad_pre_middle = (back_middle * silu_grad(pre_middle)).astype(jnp.bfloat16)
    grad_middle = weight_grad(grad_pre_middle, cols_first)
    back_first = conv_apply(columns_of(with_rims(grad_pre_middle)), flipped(weight_middle))
    grad_pre_first = (back_first * silu_grad(pre_first)).astype(jnp.bfloat16)
    grad_first = weight_grad(grad_pre_first, cols_zero)
    grad_first, grad_middle, grad_last = lax.psum(
        (grad_first, grad_middle, grad_last), ("slab", "coil", "half")
    )
    return (
        updated,
        grad_first.reshape(weight_first.shape),
        grad_middle.reshape(weight_middle.shape),
        grad_last.reshape(weight_last.shape),
    )


GROUP = ("coil", "half", "slab")


def group_sizes():
    return lax.axis_size("slab"), lax.axis_size("half"), lax.axis_size(GROUP)


def my_position():
    slab_count, half_count, _ = group_sizes()
    coil_half = lax.axis_index("coil") * half_count + lax.axis_index("half")
    return coil_half * slab_count + lax.axis_index("slab")


def device_at(position):
    slab_count, half_count, _ = group_sizes()
    coil_half = lax.div(position, slab_count)
    return {
        "slab": lax.rem(position, slab_count),
        "coil": lax.div(coil_half, half_count),
        "half": lax.rem(coil_half, half_count),
    }


def greet(count, me):
    barrier = pltpu.get_barrier_semaphore()
    for step in range(1, count):
        peer = lax.rem(me + step, count)
        pl.semaphore_signal(
            barrier, inc=1, device_id=device_at(peer), device_id_type=pl.DeviceIdType.MESH
        )
    pl.semaphore_wait(barrier, count - 1)


def send_to(src, dst, send_sem, recv_sem, peer):
    return pltpu.make_async_remote_copy(
        src_ref=src,
        dst_ref=dst,
        send_sem=send_sem,
        recv_sem=recv_sem,
        device_id=device_at(peer),
        device_id_type=pl.DeviceIdType.MESH,
    )


def scatter_slots(count, me, pick, src_ref, dst_ref, send_sem, recv_sem):
    copies = []
    for step in range(1, count):
        peer = lax.rem(me + step, count)
        copy = send_to(
            src_ref.at[pick(peer)], dst_ref.at[me], send_sem.at[step], recv_sem.at[step], peer
        )
        copy.start()
        copies.append(copy)
    dst_ref[me] = src_ref[pick(me)]
    for step in range(1, count):
        source = lax.rem(me + count - step, count)
        send_to(
            src_ref.at[pick(source)],
            dst_ref.at[source],
            send_sem.at[step],
            recv_sem.at[step],
            source,
        ).wait_recv()
    for copy in copies:
        copy.wait_send()


def exchange(values, pick, collective_id):
    _, _, count = group_sizes()

    def kernel(src_ref, dst_ref, send_sem, recv_sem):
        me = my_position()
        greet(count, me)
        scatter_slots(count, me, pick, src_ref, dst_ref, send_sem, recv_sem)

    return pl.pallas_call(
        kernel,
        out_shape=jax.ShapeDtypeStruct((count,) + values.shape[1:], values.dtype),
        in_specs=[pl.BlockSpec(memory_space=pltpu.VMEM)],
        out_specs=pl.BlockSpec(memory_space=pltpu.VMEM),
        scratch_shapes=[pltpu.SemaphoreType.DMA((count,)), pltpu.SemaphoreType.DMA((count,))],
        compiler_params=pltpu.CompilerParams(collective_id=collective_id, has_side_effects=True),
    )(values)


def total_of(values, collective_id):
    _, _, count = group_sizes()

    def kernel(src_ref, dst_ref, parts, own, send_sem, recv_sem, send_two, recv_two):
        me = my_position()
        greet(count, me)
        scatter_slots(count, me, lambda peer: peer, src_ref, parts, send_sem, recv_sem)
        own[0] = jnp.sum(parts[...], axis=0)
        scatter_slots(count, me, lambda peer: 0, own, dst_ref, send_two, recv_two)

    semaphores = pltpu.SemaphoreType.DMA((count,))
    return pl.pallas_call(
        kernel,
        out_shape=jax.ShapeDtypeStruct(values.shape, values.dtype),
        in_specs=[pl.BlockSpec(memory_space=pltpu.VMEM)],
        out_specs=pl.BlockSpec(memory_space=pltpu.VMEM),
        scratch_shapes=[
            pltpu.VMEM(values.shape, values.dtype),
            pltpu.VMEM((1,) + values.shape[1:], values.dtype),
            semaphores,
            semaphores,
            semaphores,
            semaphores,
        ],
        compiler_params=pltpu.CompilerParams(collective_id=collective_id, has_side_effects=True),
    )(values)


def dft_constants(length):
    position = np.arange(length)
    angles = (position[:, None] * position[None, :] % length) * (2.0 * math.pi / length)
    factor = 1.0 / math.sqrt(length)
    return np.cos(angles) * factor, np.sin(angles) * factor


def plane_constant(length, orient):
    cos_part, sin_part = dft_constants(length)
    return jnp.asarray(
        np.block([[cos_part, orient * sin_part], [-orient * sin_part, cos_part]]), jnp.bfloat16
    )


def lines_y(values, orient):
    return jnp.einsum(
        "cxzk,kw->cxzw",
        values,
        plane_constant(values.shape[3] // 2, orient),
        preferred_element_type=jnp.float32,
    )


def lines_z(values, orient):
    length = values.shape[2]
    half_len = values.shape[3] // 2
    cos_part, sin_part = dft_constants(length)
    mixture = jnp.einsum(
        "wz,cxzk->cxwk",
        jnp.asarray(np.concatenate([cos_part, sin_part], axis=0), jnp.bfloat16),
        values,
        preferred_element_type=jnp.float32,
    )
    direct = mixture[:, :, :length]
    crossed = mixture[:, :, length:]
    turned = jnp.concatenate(
        [-orient * crossed[..., half_len:], orient * crossed[..., :half_len]], axis=-1
    )
    return direct + turned


def band_of(x_count):
    shift = np.arange(3)[:, None, None]
    source = np.arange(x_count)[None, :, None]
    target = np.arange(x_count)[None, None, :]
    return (source == target + shift - 1).astype(np.float32)


def banded(weight, x_count):
    band = jnp.asarray(band_of(x_count), jnp.bfloat16)
    wide = jnp.einsum("dzoyi,dab->zyaibo", weight, band, preferred_element_type=jnp.bfloat16)
    return wide.reshape(3, 3, x_count * weight.shape[4], x_count * weight.shape[2])


def halves_padded(values, wide):
    half_len = values.shape[-1] // 2
    edge = [(0, 0)] * (values.ndim - 1) + [(0, wide - half_len)]
    return jnp.concatenate(
        [jnp.pad(values[..., :half_len], edge), jnp.pad(values[..., half_len:], edge)], axis=-1
    )


def two_parts(table):
    high = table.astype(ml_dtypes.bfloat16)
    low = (table - high.astype(np.float64)).astype(ml_dtypes.bfloat16)
    return jnp.asarray(high), jnp.asarray(low)


def rounded_parts(values):
    high = values.astype(jnp.bfloat16)
    return high, (values - high.astype(jnp.float32)).astype(jnp.bfloat16)


def dot(left, right):
    return jnp.dot(left, right, preferred_element_type=jnp.float32)


def images(kspace, cotangent, coil_maps, rim, collective_id):
    slab_count, _, count = group_sizes()
    coil_count, x_count, slab_rows, width = kspace.shape
    length = slab_count * slab_rows
    half_len = width // 2
    wide = -(-half_len // 128) * 128
    z_count = length // count
    window = z_count + 2 * rim
    tall = length + 2 * rim

    cos_y, sin_y = dft_constants(half_len)
    table_y = np.zeros((width, 2 * wide))
    table_y[:half_len, :half_len] = cos_y
    table_y[:half_len, wide : wide + half_len] = sin_y
    table_y[half_len:, :half_len] = -sin_y
    table_y[half_len:, wide : wide + half_len] = cos_y
    cos_z, sin_z = dft_constants(length)
    table_z = np.zeros((2 * tall, length))
    table_z[rim : rim + length] = cos_z
    table_z[tall + rim : tall + rim + length] = sin_z
    maps = halves_padded(coil_maps[:, 0], wide)
    maps = jnp.pad(maps, ((0, 0), (rim, rim), (0, 0)))

    def kernel(
        k_ref, g_ref, maps_ref, yh_ref, yl_ref, zh_ref, zl_ref, image_ref, adjoint_ref,
        moved, lines, total, slots, parts, send_one, recv_one, send_two, recv_two,
    ):
        me = my_position()
        slab = lax.axis_index("slab")
        greet(count, me)

        def moving(which, step, source_ref, sending):
            offset = step if sending else slab_count - step
            peer = lax.rem(slab + offset, slab_count)
            return pltpu.make_async_remote_copy(
                src_ref=source_ref.at[:, peer],
                dst_ref=moved.at[which, slab if sending else peer],
                send_sem=send_one.at[which, step],
                recv_sem=recv_one.at[which, step],
                device_id={"slab": peer},
                device_id_type=pl.DeviceIdType.MESH,
            )

        def spreading(which, step, sending):
            peer = lax.rem(me + (step if sending else count - step), count)
            return send_to(
                slots.at[which, peer],
                parts.at[which, me if sending else peer],
                send_two.at[which, step],
                recv_two.at[which, step],
                peer,
            )

        sources = (k_ref, g_ref)
        for which in range(2):
            for step in range(1, slab_count):
                moving(which, step, sources[which], True).start()
        for which in range(2):
            moved[which, slab] = sources[which][:, slab]
        for which in range(2):
            for step in range(1, slab_count):
                moving(which, step, sources[which], False).wait_recv()
            for block in range(slab_count):
                rows = moved[which, block].reshape(coil_count * slab_rows, width)
                product = dot(rows, yh_ref[...]) + dot(rows, yl_ref[...])
                lines[:, block * slab_rows : (block + 1) * slab_rows] = product.reshape(
                    coil_count, slab_rows, 2 * wide
                )

            @pl.loop(0, coil_count)
            def _(coil):
                high, low = rounded_parts(lines[coil])
                mixture = dot(zh_ref[...], high) + dot(zh_ref[...], low) + dot(zl_ref[...], high)
                line_real = mixture[:tall, :wide] - mixture[tall:, wide:]
                line_imag = mixture[:tall, wide:] + mixture[tall:, :wide]
                coil_map = maps_ref[coil].astype(jnp.float32)
                map_real, map_imag = coil_map[:, :wide], coil_map[:, wide:]
                real_part = map_real * line_real + map_imag * line_imag
                imag_part = map_real * line_imag - map_imag * line_real
                fresh = jnp.concatenate([real_part, imag_part], axis=1)
                total[...] = jnp.where(coil == 0, fresh, total[...] + fresh)

            for spot in range(count):
                slots[which, spot] = total[spot * z_count : spot * z_count + window].astype(
                    jnp.bfloat16
                )
            for step in range(1, count):
                spreading(which, step, True).start()
            parts[which, me] = slots[which, me]
        outs = (image_ref, adjoint_ref)
        for which in range(2):
            for step in range(1, count):
                spreading(which, step, False).wait_recv()
            for spot in range(slab_count):
                summed = parts[which, spot].astype(jnp.float32)
                for other in range(spot + slab_count, count, slab_count):
                    summed = summed + parts[which, other].astype(jnp.float32)
                summed = summed.astype(jnp.bfloat16).astype(jnp.float32)
                outs[which][:, 2 * spot, :] = summed[:, :wide]
                outs[which][:, 2 * spot + 1, :] = summed[:, wide:]
        for which in range(2):
            for step in range(1, slab_count):
                moving(which, step, sources[which], True).wait_send()
            for step in range(1, count):
                spreading(which, step, True).wait_send()

    shape = jax.ShapeDtypeStruct((window, 2 * slab_count, wide), jnp.float32)
    whole = pl.BlockSpec(memory_space=pltpu.VMEM)
    return pl.pallas_call(
        kernel,
        out_shape=(shape, shape),
        in_specs=[whole] * 7,
        out_specs=(whole, whole),
        scratch_shapes=[
            pltpu.VMEM((2, slab_count, coil_count, slab_rows, width), jnp.bfloat16),
            pltpu.VMEM((coil_count, length, 2 * wide), jnp.float32),
            pltpu.VMEM((tall, 2 * wide), jnp.float32),
            pltpu.VMEM((2, count, window, 2 * wide), jnp.bfloat16),
            pltpu.VMEM((2, count, window, 2 * wide), jnp.bfloat16),
            pltpu.SemaphoreType.DMA((2, slab_count)),
            pltpu.SemaphoreType.DMA((2, slab_count)),
            pltpu.SemaphoreType.DMA((2, count)),
            pltpu.SemaphoreType.DMA((2, count)),
        ],
        compiler_params=pltpu.CompilerParams(
            collective_id=collective_id, has_side_effects=True, vmem_limit_bytes=48 * 2**20
        ),
    )(kspace, cotangent, maps, *two_parts(table_y), *two_parts(table_z))


LANES = 128


def tap_rows(kernel):
    edge = [(0, 0), (0, 0), (0, LANES - kernel.shape[2]), (0, LANES - kernel.shape[3])]
    return jnp.pad(kernel, edge).reshape(3, 3 * LANES, LANES)


def back_taps(kernel):
    return jnp.transpose(jnp.flip(kernel, (0, 1)), (0, 1, 3, 2))


def pixels_of(plane, y_count):
    filler = jnp.zeros((LANES - plane.shape[0], plane.shape[1]), plane.dtype)
    return jnp.concatenate([plane, filler], axis=0).T[:y_count]


def fill_taps(taps_ref, row, values):
    y_count = values.shape[0]
    position = lax.broadcasted_iota(jnp.int32, values.shape, 0)
    before = jnp.where(position == 0, 0.0, pltpu.roll(values, 1, 0))
    after = jnp.where(position == y_count - 1, 0.0, pltpu.roll(values, y_count - 1, 0))
    taps_ref[row, :, :LANES] = before.astype(jnp.bfloat16)
    taps_ref[row, :, LANES : 2 * LANES] = values.astype(jnp.bfloat16)
    taps_ref[row, :, 2 * LANES :] = after.astype(jnp.bfloat16)


def conv_row(taps_ref, weight_ref, row):
    summed = dot(taps_ref[row], weight_ref[0])
    for shift_z in range(1, 3):
        summed = summed + dot(taps_ref[row + shift_z], weight_ref[shift_z])
    return summed


def row_inside(row, me, z_count, length):
    place = me * z_count + row
    return jnp.logical_and(place >= 0, place < length)


def forward_layers(image, weights, z_count, length, y_count):
    def kernel(
        image_ref, first_ref, middle_ref, last_ref,
        refined_ref, taps_zero, taps_first, taps_middle, pre_first, pre_middle,
    ):
        me = my_position()

        @pl.loop(0, z_count + 6)
        def _(row):
            fill_taps(taps_zero, row, pixels_of(image_ref[row + 1], y_count))

        @pl.loop(0, z_count + 4)
        def _(row):
            pre = conv_row(taps_zero, first_ref, row)
            pre_first[row] = pre
            act = pre / (1.0 + jnp.exp(-pre))
            fill_taps(
                taps_first, row, jnp.where(row_inside(row - 2, me, z_count, length), act, 0.0)
            )

        @pl.loop(0, z_count + 2)
        def _(row):
            pre = conv_row(taps_first, middle_ref, row)
            pre_middle[row] = pre
            act = pre / (1.0 + jnp.exp(-pre))
            fill_taps(
                taps_middle, row, jnp.where(row_inside(row - 1, me, z_count, length), act, 0.0)
            )

        @pl.loop(0, z_count)
        def _(row):
            refined_ref[row] = conv_row(taps_middle, last_ref, row).T[: refined_ref.shape[1]]

    def taps(extra):
        return jax.ShapeDtypeStruct((z_count + extra, y_count, 3 * LANES), jnp.bfloat16)

    def full(extra):
        return jax.ShapeDtypeStruct((z_count + extra, y_count, LANES), jnp.float32)

    whole = pl.BlockSpec(memory_space=pltpu.VMEM)
    return pl.pallas_call(
        kernel,
        out_shape=(
            jax.ShapeDtypeStruct((z_count, image.shape[1], y_count), jnp.float32),
            taps(6), taps(4), taps(2), full(4), full(2),
        ),
        in_specs=[whole] * 4,
        out_specs=(whole,) * 6,
        compiler_params=pltpu.CompilerParams(vmem_limit_bytes=48 * 2**20),
    )(image, *weights)


def backward_layers(
    adjoint, taps_zero, taps_first, taps_middle, pre_first, pre_middle, weights,
    z_count, length, y_count, x_count, slot_rows,
):
    channels = LANES // x_count
    few = adjoint.shape[1]

    def kernel(
        adjoint_ref, zero_ref, first_ref, middle_ref, pre_first_ref, pre_middle_ref,
        back_middle_ref, back_last_ref, out_ref, out_taps, grad_taps, sums,
    ):
        me = my_position()

        @pl.loop(0, z_count + 4)
        def _(row):
            fill_taps(out_taps, row, -pixels_of(adjoint_ref[row + 2], y_count))

        @pl.loop(0, z_count + 2)
        def _(row):
            grad = conv_row(out_taps, back_last_ref, row) * silu_grad(pre_middle_ref[row])
            fill_taps(
                grad_taps, row, jnp.where(row_inside(row - 1, me, z_count, length), grad, 0.0)
            )

        sums[...] = jnp.zeros_like(sums)

        def gather(which, grad, taps_ref, row):
            for shift_z in range(3):
                sums[which, shift_z] += lax.dot_general(
                    grad,
                    taps_ref[row + shift_z],
                    (((0,), (0,)), ((), ())),
                    preferred_element_type=jnp.float32,
                )

        @pl.loop(0, z_count)
        def _(row):
            grad = conv_row(grad_taps, back_middle_ref, row) * silu_grad(pre_first_ref[row + 2])
            gather(0, grad.astype(jnp.bfloat16), zero_ref, row + 2)
            gather(1, grad_taps[row + 1, :, LANES : 2 * LANES], first_ref, row + 1)
            gather(2, out_taps[row + 2, :, LANES : 2 * LANES], middle_ref, row)

        out_ref[...] = jnp.zeros_like(out_ref)
        group = lax.broadcasted_iota(jnp.int32, (channels, LANES), 1) // channels
        for shift_z in range(3):
            for shift_y in range(3):
                tap = shift_z * 3 + shift_y
                lanes = slice(shift_y * LANES, (shift_y + 1) * LANES)
                square = sums[1, shift_z, :, lanes]
                folded = jnp.zeros((channels, LANES), jnp.float32)
                for shift_x in range(3):
                    picked = jnp.zeros((channels, LANES), jnp.float32)
                    for spot in range(x_count):
                        picked = picked + jnp.where(
                            group == spot + shift_x - 1,
                            square[spot * channels : (spot + 1) * channels],
                            0.0,
                        )
                    turn = LANES // 2
                    while turn >= channels:
                        picked = picked + pltpu.roll(picked, turn, 1)
                        turn //= 2
                    folded = jnp.where(group == shift_x, picked, folded)
                out_ref[tap * channels : (tap + 1) * channels] = folded
                base = 9 * channels + tap * few
                out_ref[base : base + few] = sums[0, shift_z, :, lanes].T[:few]
                base = base + 9 * few
                out_ref[base : base + few] = sums[2, shift_z, :few, lanes]

    whole = pl.BlockSpec(memory_space=pltpu.VMEM)
    return pl.pallas_call(
        kernel,
        out_shape=jax.ShapeDtypeStruct((slot_rows, LANES), jnp.float32),
        in_specs=[whole] * 8,
        out_specs=whole,
        scratch_shapes=[
            pltpu.VMEM((z_count + 4, y_count, 3 * LANES), jnp.bfloat16),
            pltpu.VMEM((z_count + 2, y_count, 3 * LANES), jnp.bfloat16),
            pltpu.VMEM((3, 3, LANES, 3 * LANES), jnp.float32),
        ],
        compiler_params=pltpu.CompilerParams(vmem_limit_bytes=56 * 2**20),
    )(adjoint, taps_zero, taps_first, taps_middle, pre_first, pre_middle, *weights)


def band_sums(pairs, x_count):
    pieces = []
    for shift_x in range(3):
        picked = [
            pairs(target + shift_x - 1, target)
            for target in range(x_count)
            if 0 <= target + shift_x - 1 < x_count
        ]
        pieces.append(functools.reduce(jnp.add, picked))
    return jnp.stack(pieces)


def shards(
    kspace,
    measured,
    cotangent,
    coil_maps,
    sample_mask,
    step_size,
    weight_first,
    weight_middle,
    weight_last,
):
    slab_count, _, count = group_sizes()
    length = coil_maps.shape[2]
    half_len = kspace.shape[3] // 2
    z_count = length // count
    rim = 4
    lanes = slab_count * weight_middle.shape[2]
    if coil_maps.shape[1] != 1 or length % count or z_count % 8 or lanes != LANES or half_len % 16:
        return shards_small_chunks(
            kspace,
            measured,
            cotangent,
            coil_maps,
            sample_mask,
            step_size,
            weight_first,
            weight_middle,
            weight_last,
        )
    x_count = slab_count

    image, adjoint = images(kspace, cotangent, coil_maps, rim, 0)
    kernel_first = banded(weight_first, x_count)
    kernel_middle = banded(weight_middle, x_count)
    kernel_last = banded(weight_last, x_count)
    refined, *kept = forward_layers(
        image,
        (tap_rows(kernel_first), tap_rows(kernel_middle), tap_rows(kernel_last)),
        z_count,
        length,
        half_len,
    )
    refined = refined.astype(jnp.bfloat16).reshape(z_count, x_count, 2, half_len)
    refined = jnp.transpose(refined, (1, 0, 2, 3)).reshape(x_count, z_count * 2, half_len)
    refined_all = exchange(refined, lambda peer: lax.rem(peer, slab_count), 1)
    refined_all = refined_all.reshape(1, length, 2, half_len)

    spectra = lines_z(coil_expand(refined_all, coil_maps).astype(jnp.bfloat16), -1.0)
    spectra_slab = lax.all_to_all(
        spectra.astype(jnp.bfloat16), "slab", split_axis=2, concat_axis=1, tiled=True
    )
    model_term = lines_y(spectra_slab, -1.0)
    sampled = sample_mask.astype(jnp.float32)
    sampled = jnp.concatenate([sampled, sampled], axis=1)
    current = kspace.astype(jnp.float32)
    updated = (
        current - step_size[0] * sampled * (current - measured.astype(jnp.float32)) - model_term
    ).astype(jnp.bfloat16)

    channels = LANES // x_count
    few = 2 * x_count
    used = 9 * (channels + 2 * few)
    slot_rows = -(-used // (8 * count)) * 8 * count
    local = backward_layers(
        adjoint,
        *kept,
        (tap_rows(back_taps(kernel_middle)), tap_rows(back_taps(kernel_last))),
        z_count,
        length,
        half_len,
        x_count,
        slot_rows,
    )
    total = total_of(local.reshape(count, -1, LANES), 3).reshape(slot_rows, LANES)
    wide_rows = 9 * channels
    middle = total[:wide_rows].reshape(3, 3, channels, x_count, channels)[:, :, :, :3]
    first = total[wide_rows : wide_rows + 9 * few].reshape(3, 3, x_count, 2, x_count, channels)
    last = total[wide_rows + 9 * few : used].reshape(3, 3, x_count, 2, x_count, channels)
    grad_middle = jnp.transpose(middle, (3, 0, 2, 1, 4))
    grad_first = band_sums(lambda source, target: first[:, :, source, :, target], x_count)
    grad_last = band_sums(lambda source, target: last[:, :, target, :, source], x_count)
    return (
        updated,
        jnp.transpose(grad_first, (0, 1, 4, 2, 3)),
        grad_middle,
        jnp.transpose(grad_last, (0, 1, 3, 2, 4)),
    )


def solution(mesh):
    return jax.shard_map(
        shards,
        mesh=mesh,
        in_specs=(
            P(("grp", "coil", "half"), None, "slab", None),
            P(("grp", "coil", "half"), None, "slab", None),
            P(("grp", "coil", "half"), None, "slab", None),
            P(("grp", "coil", "half"), "slab", None, None),
            P(("grp", "slab"), None),
            P(),
            P(),
            P(),
            P(),
        ),
        out_specs=(
            P(("grp", "coil", "half"), None, "slab", None),
            P("grp", None, None, None, None),
            P("grp", None, None, None, None),
            P("grp", None, None, None, None),
        ),
        check_vma=False,
    )
```

profile of v0, /device:TPU:0, one launch (start us, length us, event | category | flops | bytes accessed | tf_op | source)
XLA Modules:
  0.0 158.9 jit_solution(4365926895008643015)
XLA Ops:
  0.6 0.0 copy-start.21
  0.6 0.0 copy-start.18
  0.7 2.2 %copy.92 = bf16[4,1,128,640]{2,3,0,1:T(8,128)(2,1)} copy(bf16[4,1,128,640]{3,2,1,0:T(8,128)(2,1)} %param.21) | data formatting | bytes 1310720 | tf_op args[3]
  2.9 0.2 slice.139
  3.2 0.5 convolution_bitcast_fusion.1
  3.7 1.0 copy.96
  4.7 0.0 copy-start.19
  4.7 0.6 reshape.314.middle_ref
  5.3 0.1 copy-done.19
  5.4 0.1 convolution_bitcast_fusion.2
  5.6 0.1 reshape.315
  5.7 0.9 copy.141
  6.6 0.1 fusion.4
  6.7 0.0 copy-start.2
  6.7 0.0 copy-start.3
  6.7 0.0 copy-start.8
  6.7 0.0 copy-start.9
  6.7 0.2 pad.24.maps_ref
  6.9 0.6 copy-done.14
  7.6 0.1 pad.26.clone
  7.6 0.1 convolution_bitcast_fusion.3
  7.8 0.7 copy.94
  8.4 1.6 %reshape.312 = bf16[3,3,8,128]{3,2,1,0:T(8,128)(2,1)} reshape(bf16[3,3,4,2,4,32]{5,4,3,2,1,0:T(4,128)(2,1)} %copy.94) | data formatting | bytes 36864 | tf_op jit(solution)/shard_map/reshape | solution.py:387
  10.0 0.8 pad.25
  10.9 1.1 copy-done.4
  12.0 1.1 copy-done.5
  13.0 53.1 %shard_map.201 = (f32[16,8,384]{2,1,0:T(8,128)S(1)}, f32[16,8,384]{2,1,0:T(8,128)S(1)}) custom-call(bf16[4,4,32,640]{3,2,1,0:T(8,128)(2,1)S(1)} %copy-done.5, bf16[4,4,32,640]{3,2,1,0:T(8,128)(2,1)S(1)} %copy-done.4, bf16[4,136,768]{2,1,0:T(8,128)(2,1)S(1)} %pad.24.maps_ref, bf16[640,768]{1,0:T(8,128)(2,1)S(1)} %copy-done.2, bf16[640,768]{1,0:T(8,128)(2,1)S(1)} %copy-done.3, ...), custom_call_target="tpu_custom_call" | custom-call | tf_op jit(solution)/shard_map/pallas_call | solution.py:521
  66.1 0.7 copy-done.7
  66.8 17.3 %shard_map.202 = (f32[8,8,320]{2,1,0:T(8,128)S(1)}, bf16[14,320,384]{2,1,0:T(8,128)(2,1)}, bf16[12,320,384]{2,1,0:T(8,128)(2,1)}, bf16[10,320,384]{2,1,0:T(8,128...) custom-call(f32[16,8,384]{2,1,0:T(8,128)S(1)} %get-tuple-element.12.image_ref, ...), custom_call_target="tpu_custom_call" | custom-call | tf_op jit(solution)/shard_map/pallas_call | solution.py:622
  84.1 1.3 copy-done
  85.4 1.2 copy-done.1
  86.7 0.7 reshape.318.src_ref
  87.3 10.4 %shard_map.203 = bf16[16,16,320]{2,1,0:T(8,128)(2,1)} custom-call(bf16[4,16,320]{2,1,0:T(8,128)(2,1)} %reshape.318.src_ref), custom_call_target="tpu_custom_call" | custom-call | tf_op jit(solution)/shard_map/pallas_call | solution.py:298
  97.8 1.0 reshape.319
  98.8 0.3 fusion.19
  99.1 0.2 copy.124
  99.3 0.2 copy.125
  99.4 0.1 convert_element_type.62
  99.5 0.0 copy-start.16
  99.6 0.2 fusion.8
  99.8 0.6 copy-done.16
  100.4 0.5 convolution_bitcast_fusion
  100.9 0.1 fusion.17
  101.0 0.1 fusion.3
  101.1 1.3 copy.103
  102.4 3.7 %all-to-all-start = ((bf16[4,1,128,640]{3,0,1,2:T(4,128)(2,1)}), bf16[4,1,128,640]{3,0,1,2:T(4,128)(2,1)S(1)}, u32[]{:S(2)}, u32[]{:S(2)}) async-start(bf16[4,1,128,640]{3,0,1,2:T(4,128)(2,1)} %copy.103), calls=%async_computation | async-start | bytes 1310720 | tf_op jit(solution)/shard_map/all_to_all | solution.py:778
  106.1 0.6 reshape.320
  106.7 0.9 copy.106
  107.6 0.8 pad.27
  108.4 21.0 %shard_map.204 = f32[512,128]{1,0:T(8,128)} custom-call(f32[16,8,384]{2,1,0:T(8,128)} %copy-done.7, bf16[14,320,384]{2,1,0:T(8,128)(2,1)} %get-tuple-element.15.zero_ref, bf16[12,320,384]{2,1,0:T(8,128)(2,1)} %get-tuple-element.16.first_ref, bf16[10,320,384]{2,1,0:T(8,128)(2,1)} %get-tuple-element.17.middle_ref, f32[12,320,128]{2,1,0:T(8,128)} %copy-done, ...), custom_call_target="tpu_custom_call" | custom-call | tf_op jit(solution)/shard_map/pallas_call | solution.py:704
  129.4 21.3 %shard_map.205 = f32[16,32,128]{2,1,0:T(8,128)} custom-call(f32[16,32,128]{2,1,0:T(8,128)} %bitcast.100), custom_call_target="tpu_custom_call" | custom-call | tf_op jit(solution)/shard_map/pallas_call | solution.py:319
  150.7 0.9 slice.124
  151.6 0.8 fusion.18
  152.4 0.1 reshape.327
  152.6 0.1 fusion.20
  152.6 0.1 reshape.325
  153.4 0.3 reshape.326
  153.8 0.8 copy.156
  154.6 0.6 maximum_bitcast_fusion.1
  155.2 0.1 fusion.21
  155.3 0.6 maximum_bitcast_fusion
  155.9 0.1 maximum_multiply_fusion
  156.0 0.1 copy.104
  156.1 2.7 %fusion.1 = bf16[4,4,32,640]{3,2,1,0:T(8,128)(2,1)} fusion(bf16[4,4,32,640]{3,2,1,0:T(8,128)(2,1)S(1)} %bitcast.102, bf16[640,640,1,1]{1,0,3,2:T(8,128)(2,1)} %constant.44, bf16[4,4,32,640]{3,2,1,0:T(8,128)(2,1)S(1)} %copy-done.6, bf16[4,4,32,640]{3,2,1,0:T(8,128)(2,1)S(1)} %copy-done.22, f32[32,640]{1,0:T(8,128)S(1)} %maximum_multiply_fusion), kind=kOutput, calls=%fused_computation.7 | convolution fusion | flops 421724160 | bytes 3522560 | tf_op jit(solution)/shard_map/cxzk,kw->cxzw/dot_general | solution.py:351
  (42 shorter events, 0.3 us)
Async XLA Ops:
  0.6 2.5 %copy-start.21 = (pred[384]{0:T(512)(128)(4,1)S(1)}, pred[384]{0:T(512)(128)(4,1)}, u32[]{:S(2)}) copy-start(pred[384]{0:T(512)(128)(4,1)} %constant.18.clone.1) | copy-start | bytes 1156
  0.6 2.5 %copy-start.18 = (bf16[3,4,4,1,1,1]{0,2,5,4,3,1:T(4,128)(2,1)S(1)}, bf16[3,4,4,1,1,1]{0,2,5,4,3,1:T(4,128)(2,1)}, u32[]{:S(2)}) copy-start(bf16[3,4,4,1,1,1]{0,2,5,4,3,1:T(4,128)(2,1)} %constant.42) | copy-start | bytes 292
  0.7 2.3 %copy-start.12 = (bf16[4,1,128,640]{3,2,1,0:T(8,128)(2,1)S(1)}, bf16[4,1,128,640]{3,2,1,0:T(8,128)(2,1)}, u32[]{:S(2)}) copy-start(bf16[4,1,128,640]{3,2,1,0:T(8,128)(2,1)} %param.21) | copy-start | bytes 1966084
  0.7 2.5 %copy-start.15 = (bf16[3,3,32,3,32]{4,2,3,1,0:T(8,128)(2,1)S(1)}, bf16[3,3,32,3,32]{4,2,3,1,0:T(8,128)(2,1)}, u32[]{:S(2)}) copy-start(bf16[3,3,32,3,32]{4,2,3,1,0:T(8,128)(2,1)} %param.25) | copy-start | bytes 165892
  4.7 1.9 %copy-start.10 = (bf16[3,3,4,32,4,32]{5,4,3,2,1,0:T(4,128)(2,1)}, bf16[3,3,4,32,4,32]{5,4,3,2,1,0:T(4,128)(2,1)S(1)}, u32[]{:S(2)}) copy-start(bf16[3,3,4,32,4,32]{5,4,3,2,1,0:T(4,128)(2,1)S(1)} %copy.96) | copy-start | bytes 884740
  4.7 0.7 copy-start.19
  6.6 1.0 copy-start.14
  6.7 0.9 copy-start.20
  6.7 4.1 %copy-start.2 = (bf16[640,768]{1,0:T(8,128)(2,1)S(1)}, bf16[640,768]{1,0:T(8,128)(2,1)}, u32[]{:S(2)}) copy-start(bf16[640,768]{1,0:T(8,128)(2,1)} %constant.21.clone.yh_ref) | copy-start | bytes 2949124
  6.7 4.1 %copy-start.3 = (bf16[640,768]{1,0:T(8,128)(2,1)S(1)}, bf16[640,768]{1,0:T(8,128)(2,1)}, u32[]{:S(2)}) copy-start(bf16[640,768]{1,0:T(8,128)(2,1)} %constant.22.clone.yl_ref) | copy-start | bytes 2949124
  6.7 4.1 %copy-start.8 = (bf16[272,128]{1,0:T(8,128)(2,1)S(1)}, bf16[272,128]{1,0:T(8,128)(2,1)}, u32[]{:S(2)}) copy-start(bf16[272,128]{1,0:T(8,128)(2,1)} %constant.23.clone.zh_ref) | copy-start | bytes 208900
  6.7 4.1 %copy-start.9 = (bf16[272,128]{1,0:T(8,128)(2,1)S(1)}, bf16[272,128]{1,0:T(8,128)(2,1)}, u32[]{:S(2)}) copy-start(bf16[272,128]{1,0:T(8,128)(2,1)} %constant.24.clone.zl_ref) | copy-start | bytes 208900
  10.9 1.1 copy-start.4
  11.9 1.1 copy-start.5
  66.1 0.7 copy-start.7
  84.1 1.3 copy-start
  85.4 1.2 copy-start.1
  86.6 12.9 %copy-start.13 = (bf16[4,1,128,640]{2,3,0,1:T(8,128)(2,1)S(1)}, bf16[4,1,128,640]{2,3,0,1:T(8,128)(2,1)}, u32[]{:S(2)}) copy-start(bf16[4,1,128,640]{2,3,0,1:T(8,128)(2,1)} %copy.92) | copy-start | bytes 1966084
  99.5 0.8 copy-start.16
  101.1 5.0 %copy-start.11 = (bf16[3,3,4,32,4,32]{5,4,3,2,1,0:T(4,128)(2,1)S(1)}, bf16[3,3,4,32,4,32]{5,4,3,2,1,0:T(4,128)(2,1)}, u32[]{:S(2)}) copy-start(bf16[3,3,4,32,4,32]{5,4,3,2,1,0:T(4,128)(2,1)} %copy-done.10) | copy-start | bytes 884740
  102.4 53.6 %all-to-all-start = ((bf16[4,1,128,640]{3,0,1,2:T(4,128)(2,1)}), bf16[4,1,128,640]{3,0,1,2:T(4,128)(2,1)S(1)}, u32[]{:S(2)}, u32[]{:S(2)}) async-start(bf16[4,1,128,640]{3,0,1,2:T(4,128)(2,1)} %copy.103), calls=%async_computation | async-start | bytes 1310720 | tf_op jit(solution)/shard_map/all_to_all | solution.py:778
  129.4 23.4 %copy-start.17 = (s32[32,320]{1,0:T(8,128)S(1)}, s32[32,320]{1,0:T(8,128)}, u32[]{:S(2)}) copy-start(s32[32,320]{1,0:T(8,128)} %param.22) | copy-start | bytes 122884
  153.7 2.4 %copy-start.6 = (bf16[4,4,32,640]{3,2,1,0:T(8,128)(2,1)S(1)}, bf16[4,4,32,640]{3,2,1,0:T(8,128)(2,1)}, u32[]{:S(2)}) copy-start(bf16[4,4,32,640]{3,2,1,0:T(8,128)(2,1)} %k_ref.1) | copy-start | bytes 1966084
  153.8 2.4 %copy-start.22 = (bf16[4,4,32,640]{3,2,1,0:T(8,128)(2,1)S(1)}, bf16[4,4,32,640]{3,2,1,0:T(8,128)(2,1)}, u32[]{:S(2)}) copy-start(bf16[4,4,32,640]{3,2,1,0:T(8,128)(2,1)} %param.19) | copy-start | bytes 1966084
where the time goes:
time: 160 us; the launch traced here: 159 us
  Pallas kernels  123 us (77%)
  local copies, waits for them, and re-layouts  24.1 us (15%)
  matrix products  4.01 us (3%)
  starting transfers between devices  3.66 us (2%)
  other arithmetic  2.15 us (1%)
  between operations  1.8 us (1%)
    pallas_call x1, Pallas kernels, images(): pl.pallas_call(kernel, out_shape=(shape, shape), in_specs=[whole] * 7, ou...  53.1 us
    pallas_call x1, Pallas kernels, total_of(): pl.pallas_call(kernel, out_shape=jax.ShapeDtypeStruct(values.shape, value...  21.3 us
    pallas_call x1, Pallas kernels, backward_layers(): pl.pallas_call(kernel, out_shape=jax.ShapeDtypeStruct((slot_rows, LANES),...  21 us
    pallas_call x1, Pallas kernels, forward_layers(): pl.pallas_call(kernel, out_shape=(jax.ShapeDtypeStruct((z_count, image.sh...  17.3 us
    unnamed x51, local copies, waits for them, and re-layouts  11.1 us
    pallas_call x1, Pallas kernels, exchange(): pl.pallas_call(kernel, out_shape=jax.ShapeDtypeStruct((count,) + values.s...  10.4 us
    all_to_all x1, starting transfers between devices, shards(): lax.all_to_all(spectra.astype(jnp.bfloat16), 'slab', split_axis=2, concat...  3.66 us
  transfers between devices with their start and end apart: 1, of which 0 were waited for; matrix products, arithmetic and copies ran while one was open for 4% of the time, Pallas kernels for 27%

commit v1 on v0

--- a/solution.py
+++ b/solution.py
@@ -287,24 +287,6 @@
         copy.wait_send()
 
 
-def exchange(values, pick, collective_id):
-    _, _, count = group_sizes()
-
-    def kernel(src_ref, dst_ref, send_sem, recv_sem):
-        me = my_position()
-        greet(count, me)
-        scatter_slots(count, me, pick, src_ref, dst_ref, send_sem, recv_sem)
-
-    return pl.pallas_call(
-        kernel,
-        out_shape=jax.ShapeDtypeStruct((count,) + values.shape[1:], values.dtype),
-        in_specs=[pl.BlockSpec(memory_space=pltpu.VMEM)],
-        out_specs=pl.BlockSpec(memory_space=pltpu.VMEM),
-        scratch_shapes=[pltpu.SemaphoreType.DMA((count,)), pltpu.SemaphoreType.DMA((count,))],
-        compiler_params=pltpu.CompilerParams(collective_id=collective_id, has_side_effects=True),
-    )(values)
-
-
 def total_of(values, collective_id):
     _, _, count = group_sizes()
 
@@ -312,7 +294,7 @@
         me = my_position()
         greet(count, me)
         scatter_slots(count, me, lambda peer: peer, src_ref, parts, send_sem, recv_sem)
-        own[0] = jnp.sum(parts[...], axis=0)
+        own[0] = jnp.sum(parts[...].astype(jnp.float32), axis=0).astype(own.dtype)
         scatter_slots(count, me, lambda peer: 0, own, dst_ref, send_two, recv_two)
 
     semaphores = pltpu.SemaphoreType.DMA((count,))
@@ -410,7 +392,7 @@
     return jnp.dot(left, right, preferred_element_type=jnp.float32)
 
 
-def images(kspace, cotangent, coil_maps, rim, collective_id):
+def images(kspace, cotangent, coil_maps, weights, rim, collective_id):
     slab_count, _, count = group_sizes()
     coil_count, x_count, slab_rows, width = kspace.shape
     length = slab_count * slab_rows
@@ -434,8 +416,10 @@
     maps = jnp.pad(maps, ((0, 0), (rim, rim), (0, 0)))
 
     def kernel(
-        k_ref, g_ref, maps_ref, yh_ref, yl_ref, zh_ref, zl_ref, image_ref, adjoint_ref,
-        moved, lines, total, slots, parts, send_one, recv_one, send_two, recv_two,
+        k_ref, g_ref, maps_ref, yh_ref, yl_ref, zh_ref, zl_ref, first_ref, middle_ref, last_ref,
+        adjoint_ref, refined_ref, taps_zero, taps_first, taps_middle, pre_first, pre_middle,
+        image_ref, moved, lines, total, slots, parts, planes, stacked, refined_slots,
+        send_one, recv_one, send_two, recv_two, send_three, recv_three,
     ):
         me = my_position()
         slab = lax.axis_index("slab")
@@ -464,12 +448,24 @@
             )
 
         sources = (k_ref, g_ref)
-        for which in range(2):
+        outs = (image_ref, adjoint_ref)
+
+        def refining(step, sending):
+            peer = lax.rem(me + (step if sending else count - step), count)
+            return send_to(
+                refined_slots.at[lax.rem(peer, slab_count)],
+                refined_ref.at[me if sending else peer],
+                send_three.at[step],
+                recv_three.at[step],
+                peer,
+            )
+
+        def start_moving(which):
             for step in range(1, slab_count):
                 moving(which, step, sources[which], True).start()
-        for which in range(2):
             moved[which, slab] = sources[which][:, slab]
-        for which in range(2):
+
+        def start_spreading(which):
             for step in range(1, slab_count):
                 moving(which, step, sources[which], False).wait_recv()
             for block in range(slab_count):
@@ -499,8 +495,8 @@
             for step in range(1, count):
                 spreading(which, step, True).start()
             parts[which, me] = slots[which, me]
-        outs = (image_ref, adjoint_ref)
-        for which in range(2):
+
+        def finish_spreading(which):
             for step in range(1, count):
                 spreading(which, step, False).wait_recv()
             for spot in range(slab_count):
@@ -510,34 +506,95 @@
                 summed = summed.astype(jnp.bfloat16).astype(jnp.float32)
                 outs[which][:, 2 * spot, :] = summed[:, :wide]
                 outs[which][:, 2 * spot + 1, :] = summed[:, wide:]
+
+        start_moving(0)
+        start_spreading(0)
+        start_moving(1)
+        finish_spreading(0)
+
+        @pl.loop(0, z_count + 6)
+        def _(row):
+            fill_taps(taps_zero, row, pixels_of(image_ref[row + 1], half_len))
+
+        @pl.loop(0, z_count + 4)
+        def _(row):
+            pre = conv_row(taps_zero, first_ref, row)
+            pre_first[row] = pre
+            act = pre / (1.0 + jnp.exp(-pre))
+            fill_taps(
+                taps_first, row, jnp.where(row_inside(row - 2, me, z_count, length), act, 0.0)
+            )
+
+        @pl.loop(0, z_count + 2)
+        def _(row):
+            pre = conv_row(taps_first, middle_ref, row)
+            pre_middle[row] = pre
+            act = pre / (1.0 + jnp.exp(-pre))
+            fill_taps(
+                taps_middle, row, jnp.where(row_inside(row - 1, me, z_count, length), act, 0.0)
+            )
+
+        @pl.loop(0, z_count)
+        def _(row):
+            planes[row] = conv_row(taps_middle, last_ref, row).T[: 2 * slab_count]
+
+        for spot in range(slab_count):
+            for row in range(z_count):
+                stacked[spot, 2 * row : 2 * row + 2] = planes[row, 2 * spot : 2 * spot + 2]
+            refined_slots[spot] = stacked[spot].astype(jnp.bfloat16)
+        for step in range(1, count):
+            refining(step, True).start()
+        refined_ref[me] = refined_slots[slab]
+        start_spreading(1)
+        for step in range(1, count):
+            refining(step, False).wait_recv()
+        finish_spreading(1)
         for which in range(2):
             for step in range(1, slab_count):
                 moving(which, step, sources[which], True).wait_send()
             for step in range(1, count):
                 spreading(which, step, True).wait_send()
+        for step in range(1, count):
+            refining(step, True).wait_send()
+
+    def taps(extra):
+        return jax.ShapeDtypeStruct((z_count + extra, half_len, 3 * LANES), jnp.bfloat16)
+
+    def full(extra):
+        return jax.ShapeDtypeStruct((z_count + extra, half_len, LANES), jnp.float32)
 
     shape = jax.ShapeDtypeStruct((window, 2 * slab_count, wide), jnp.float32)
     whole = pl.BlockSpec(memory_space=pltpu.VMEM)
     return pl.pallas_call(
         kernel,
-        out_shape=(shape, shape),
-        in_specs=[whole] * 7,
-        out_specs=(whole, whole),
+        out_shape=(
+            shape,
+            jax.ShapeDtypeStruct((count, 2 * z_count, half_len), jnp.bfloat16),
+            taps(6), taps(4), taps(2), full(4), full(2),
+        ),
+        in_specs=[whole] * 10,
+        out_specs=(whole,) * 7,
         scratch_shapes=[
+            pltpu.VMEM((window, 2 * slab_count, wide), jnp.float32),
             pltpu.VMEM((2, slab_count, coil_count, slab_rows, width), jnp.bfloat16),
             pltpu.VMEM((coil_count, length, 2 * wide), jnp.float32),
             pltpu.VMEM((tall, 2 * wide), jnp.float32),
             pltpu.VMEM((2, count, window, 2 * wide), jnp.bfloat16),
             pltpu.VMEM((2, count, window, 2 * wide), jnp.bfloat16),
+            pltpu.VMEM((z_count, 2 * slab_count, half_len), jnp.float32),
+            pltpu.VMEM((slab_count, 2 * z_count, half_len), jnp.float32),
+            pltpu.VMEM((slab_count, 2 * z_count, half_len), jnp.bfloat16),
             pltpu.SemaphoreType.DMA((2, slab_count)),
             pltpu.SemaphoreType.DMA((2, slab_count)),
             pltpu.SemaphoreType.DMA((2, count)),
             pltpu.SemaphoreType.DMA((2, count)),
+            pltpu.SemaphoreType.DMA((count,)),
+            pltpu.SemaphoreType.DMA((count,)),
         ],
         compiler_params=pltpu.CompilerParams(
-            collective_id=collective_id, has_side_effects=True, vmem_limit_bytes=48 * 2**20
+            collective_id=collective_id, has_side_effects=True, vmem_limit_bytes=56 * 2**20
         ),
-    )(kspace, cotangent, maps, *two_parts(table_y), *two_parts(table_z))
+    )(kspace, cotangent, maps, *two_parts(table_y), *two_parts(table_z), *weights)
 
 
 LANES = 128
@@ -579,58 +636,6 @@
     return jnp.logical_and(place >= 0, place < length)
 
 
-def forward_layers(image, weights, z_count, length, y_count):
-    def kernel(
-        image_ref, first_ref, middle_ref, last_ref,
-        refined_ref, taps_zero, taps_first, taps_middle, pre_first, pre_middle,
-    ):
-        me = my_position()
-
-        @pl.loop(0, z_count + 6)
-        def _(row):
-            fill_taps(taps_zero, row, pixels_of(image_ref[row + 1], y_count))
-
-        @pl.loop(0, z_count + 4)
-        def _(row):
-            pre = conv_row(taps_zero, first_ref, row)
-            pre_first[row] = pre
-            act = pre / (1.0 + jnp.exp(-pre))
-            fill_taps(
-                taps_first, row, jnp.where(row_inside(row - 2, me, z_count, length), act, 0.0)
-            )
-
-        @pl.loop(0, z_count + 2)
-        def _(row):
-            pre = conv_row(taps_first, middle_ref, row)
-            pre_middle[row] = pre
-            act = pre / (1.0 + jnp.exp(-pre))
-            fill_taps(
-                taps_middle, row, jnp.where(row_inside(row - 1, me, z_count, length), act, 0.0)
-            )
-
-        @pl.loop(0, z_count)
-        def _(row):
-            refined_ref[row] = conv_row(taps_middle, last_ref, row).T[: refined_ref.shape[1]]
-
-    def taps(extra):
-        return jax.ShapeDtypeStruct((z_count + extra, y_count, 3 * LANES), jnp.bfloat16)
-
-    def full(extra):
-        return jax.ShapeDtypeStruct((z_count + extra, y_count, LANES), jnp.float32)
-
-    whole = pl.BlockSpec(memory_space=pltpu.VMEM)
-    return pl.pallas_call(
-        kernel,
-        out_shape=(
-            jax.ShapeDtypeStruct((z_count, image.shape[1], y_count), jnp.float32),
-            taps(6), taps(4), taps(2), full(4), full(2),
-        ),
-        in_specs=[whole] * 4,
-        out_specs=(whole,) * 6,
-        compiler_params=pltpu.CompilerParams(vmem_limit_bytes=48 * 2**20),
-    )(image, *weights)
-
-
 def backward_layers(
     adjoint, taps_zero, taps_first, taps_middle, pre_first, pre_middle, weights,
     z_count, length, y_count, x_count, slot_rows,
@@ -640,7 +645,7 @@
 
     def kernel(
         adjoint_ref, zero_ref, first_ref, middle_ref, pre_first_ref, pre_middle_ref,
-        back_middle_ref, back_last_ref, out_ref, out_taps, grad_taps, sums,
+        back_middle_ref, back_last_ref, rounded_ref, out_taps, grad_taps, sums, out_ref,
     ):
         me = my_position()
 
@@ -699,17 +704,19 @@
                 out_ref[base : base + few] = sums[0, shift_z, :, lanes].T[:few]
                 base = base + 9 * few
                 out_ref[base : base + few] = sums[2, shift_z, :few, lanes]
+        rounded_ref[...] = out_ref[...].astype(jnp.bfloat16)
 
     whole = pl.BlockSpec(memory_space=pltpu.VMEM)
     return pl.pallas_call(
         kernel,
-        out_shape=jax.ShapeDtypeStruct((slot_rows, LANES), jnp.float32),
+        out_shape=jax.ShapeDtypeStruct((slot_rows, LANES), jnp.bfloat16),
         in_specs=[whole] * 8,
         out_specs=whole,
         scratch_shapes=[
             pltpu.VMEM((z_count + 4, y_count, 3 * LANES), jnp.bfloat16),
             pltpu.VMEM((z_count + 2, y_count, 3 * LANES), jnp.bfloat16),
             pltpu.VMEM((3, 3, LANES, 3 * LANES), jnp.float32),
+            pltpu.VMEM((slot_rows, LANES), jnp.float32),
         ],
         compiler_params=pltpu.CompilerParams(vmem_limit_bytes=56 * 2**20),
     )(adjoint, taps_zero, taps_first, taps_middle, pre_first, pre_middle, *weights)
@@ -758,20 +765,20 @@
         )
     x_count = slab_count
 
-    image, adjoint = images(kspace, cotangent, coil_maps, rim, 0)
-    kernel_first = banded(weight_first, x_count)
     kernel_middle = banded(weight_middle, x_count)
     kernel_last = banded(weight_last, x_count)
-    refined, *kept = forward_layers(
-        image,
-        (tap_rows(kernel_first), tap_rows(kernel_middle), tap_rows(kernel_last)),
-        z_count,
-        length,
-        half_len,
-    )
-    refined = refined.astype(jnp.bfloat16).reshape(z_count, x_count, 2, half_len)
-    refined = jnp.transpose(refined, (1, 0, 2, 3)).reshape(x_count, z_count * 2, half_len)
-    refined_all = exchange(refined, lambda peer: lax.rem(peer, slab_count), 1)
+    adjoint, refined_all, *kept = images(
+        kspace,
+        cotangent,
+        coil_maps,
+        (
+            tap_rows(banded(weight_first, x_count)),
+            tap_rows(kernel_middle),
+            tap_rows(kernel_last),
+        ),
+        rim,
+        0,
+    )
     refined_all = refined_all.reshape(1, length, 2, half_len)
 
     spectra = lines_z(coil_expand(refined_all, coil_maps).astype(jnp.bfloat16), -1.0)
@@ -789,7 +796,7 @@
     channels = LANES // x_count
     few = 2 * x_count
     used = 9 * (channels + 2 * few)
-    slot_rows = -(-used // (8 * count)) * 8 * count
+    slot_rows = -(-used // (16 * count)) * 16 * count
     local = backward_layers(
         adjoint,
         *kept,
@@ -800,7 +807,8 @@
         x_count,
         slot_rows,
     )
-    total = total_of(local.reshape(count, -1, LANES), 3).reshape(slot_rows, LANES)
+    total = total_of(local.reshape(count, -1, LANES), 3)
+    total = total.reshape(slot_rows, LANES).astype(jnp.float32)
     wide_rows = 9 * channels
     middle = total[:wide_rows].reshape(3, 3, channels, x_count, channels)[:, :, :, :3]
     first = total[wide_rows : wide_rows + 9 * few].reshape(3, 3, x_count, 2, x_count, channels)

time: 160 us -> 136 us (0.85)
  Pallas kernels: 123 us -> 109 us
  local copies, waits for them, and re-layouts: 24.1 us -> 15.4 us
  other arithmetic: 2.15 us -> 3.82 us
    pallas_call x3 -> x1, Pallas kernels: 80.8 us -> 71 us  [images(): pl.pallas_call(kernel, out_shape=(shape, jax.ShapeDtypeStruct((count, 2 *...]
    unnamed x51 -> x29, local copies, waits for them, and re-layouts: 11.1 us -> 3.57 us
    pallas_call x1, Pallas kernels: 21.3 us -> 16.2 us  [total_of(): pl.pallas_call(kernel, out_shape=jax.ShapeDtypeStruct(values.shape, value...]
  transfers between devices with their start and end apart: 1 -> 1, of which waited for: 0 -> 0; matrix products, arithmetic and copies ran while one was open for 4% -> 5% of each run, Pallas kernels for 27% -> 28%
where the time goes in v1:
time: 136 us
  Pallas kernels  109 us (80%)
  local copies, waits for them, and re-layouts  15.4 us (11%)
  other arithmetic  3.82 us (3%)
  starting transfers between devices  3.66 us (3%)
  matrix products  2.86 us (2%)
  between operations  1.68 us (1%)
    pallas_call x1, Pallas kernels, images(): pl.pallas_call(kernel, out_shape=(shape, jax.ShapeDtypeStruct((count, 2 *...  71 us
    pallas_call x1, Pallas kernels, backward_layers(): pl.pallas_call(kernel, out_shape=jax.ShapeDtypeStruct((slot_rows, LANES),...  21.4 us
    pallas_call x1, Pallas kernels, total_of(): pl.pallas_call(kernel, out_shape=jax.ShapeDtypeStruct(values.shape, value...  16.2 us
    all_to_all x1, starting transfers between devices, shards(): lax.all_to_all(spectra.astype(jnp.bfloat16), 'slab', split_axis=2, concat...  3.66 us
    unnamed x29, local copies, waits for them, and re-layouts  3.57 us
  transfers between devices with their start and end apart: 1, of which 0 were waited for; matrix products, arithmetic and copies ran while one was open for 5% of the time, Pallas kernels for 28%

profile of v1, /device:TPU:0, one launch (start us, length us, event | category | flops | bytes accessed | tf_op | source)
XLA Modules:
  0.0 136.1 jit_solution(16896209842985231828)
XLA Ops:
  0.6 0.0 copy-start.9
  0.6 0.0 copy-start.6
  0.7 0.0 copy-start
  0.7 0.0 copy-start.3
  0.7 1.5 %copy.89 = bf16[4,1,128,640]{2,3,0,1:T(8,128)(2,1)S(1)} copy(bf16[4,1,128,640]{3,2,1,0:T(8,128)(2,1)} %param.21) | data formatting | bytes 1310720 | tf_op args[3]
  2.2 0.0 copy-done
  2.2 0.2 slice.139
  2.4 0.0 copy-done.9
  2.4 0.8 slice_select_fusion
  3.2 0.0 copy-done.6
  3.2 0.0 copy-done.3
  3.2 0.5 convolution_bitcast_fusion.1
  3.7 1.0 copy.93
  4.6 0.0 copy-start.7
  4.7 0.0 copy-start.1
  4.7 1.3 reshape.307.middle_ref
  6.0 0.0 copy-done.7
  6.0 0.1 convolution_bitcast_fusion.2
  6.2 0.1 reshape.308
  6.3 0.2 copy.137
  6.5 0.0 copy-done.1
  6.5 0.1 fusion.4
  6.6 0.0 copy-start.8
  6.6 1.2 pad.24.maps_ref
  7.8 0.8 pad.26.clone
  8.5 0.0 copy-done.8
  8.5 0.1 convolution_bitcast_fusion.3
  8.7 0.1 reshape.305
  8.8 0.8 pad.25
  9.6 71.0 %shard_map.201 = (f32[16,8,384]{2,1,0:T(8,128)}, bf16[16,16,320]{2,1,0:T(8,128)(2,1)}, bf16[14,320,384]{2,1,0:T(8,128)(2,1)}, bf16[12,320,384]{2,1,0:T(8,128)(2,...) custom-call(bf16[4,4,32,640]{3,2,1,0:T(8,128)(2,1)} %k_ref.1, ...), custom_call_target="tpu_custom_call" | custom-call | tf_op jit(solution)/shard_map/pallas_call | solution.py:568
  80.6 1.0 reshape.310
  81.7 0.3 fusion.19
  81.9 0.2 copy.120
  82.1 0.2 copy.121
  82.3 0.1 convert_element_type.65
  82.4 0.0 copy-start.4
  82.4 0.2 fusion.8
  82.6 0.6 copy-done.4
  83.2 0.5 convolution_bitcast_fusion
  83.7 0.1 fusion.17
  83.8 0.1 fusion.3
  84.0 1.3 copy.99
  85.3 3.7 %all-to-all-start = ((bf16[4,1,128,640]{3,0,1,2:T(4,128)(2,1)}), bf16[4,1,128,640]{3,0,1,2:T(4,128)(2,1)S(1)}, u32[]{:S(2)}, u32[]{:S(2)}) async-start(bf16[4,1,128,640]{3,0,1,2:T(4,128)(2,1)} %copy.99), calls=%async_computation | async-start | bytes 1310720 | tf_op jit(solution)/shard_map/all_to_all | solution.py:785
  89.0 0.6 reshape.311
  89.6 0.9 copy.102
  90.5 0.8 pad.27
  91.3 21.4 %shard_map.202 = bf16[512,128]{1,0:T(8,128)(2,1)} custom-call(f32[16,8,384]{2,1,0:T(8,128)} %get-tuple-element.12.adjoint_ref, bf16[14,320,384]{2,1,0:T(8,128)(2,1)} %get-tuple-element.13.zero_ref, bf16[12,320,384]{2,1,0:T(8,128)(2,1)} %get-tuple-element.14.first_ref, bf16[10,320,384]{2,1,0:T(8,128)(2,1)} %get-tuple-element.15.middle_ref, ...), custom_call_target="tpu_custom_call" | custom-call | tf_op jit(solution)/shard_map/pallas_call | solution.py:710
  112.7 16.2 %shard_map.203 = bf16[16,32,128]{2,1,0:T(8,128)(2,1)} custom-call(bf16[16,32,128]{2,1,0:T(8,128)(2,1)} %bitcast.98), custom_call_target="tpu_custom_call" | custom-call | tf_op jit(solution)/shard_map/pallas_call | solution.py:301
  129.0 0.9 convert_element_type.72
  129.9 0.9 slice.157
  130.8 0.1 reshape.317
  130.9 0.1 fusion.20
  131.0 0.1 reshape.315
  131.8 0.3 reshape.316
  132.1 0.0 copy-start.2
  132.1 0.0 copy-start.10
  132.1 0.8 copy.151
  133.0 0.6 maximum_bitcast_fusion.1
  133.6 0.1 fusion.21
  133.7 0.6 maximum_bitcast_fusion
  134.3 0.1 maximum_multiply_fusion
  134.4 0.0 all-to-all-done
  134.4 0.1 copy.100
  134.5 1.6 %fusion.1 = bf16[4,4,32,640]{3,2,1,0:T(8,128)(2,1)} fusion(bf16[4,4,32,640]{3,2,1,0:T(8,128)(2,1)S(1)} %bitcast.97, bf16[640,640,1,1]{1,0,3,2:T(8,128)(2,1)S(1)} %copy-done.11, bf16[4,4,32,640]{3,2,1,0:T(8,128)(2,1)S(1)} %copy-done.2, bf16[4,4,32,640]{3,2,1,0:T(8,128)(2,1)S(1)} %copy-done.10, f32[32,640]{1,0:T(8,128)S(1)} %maximum_multiply_fusion), kind=kOutput, calls=%fused_computation.7 | convolution fusion | flops 421724160 | bytes 3522560 | tf_op jit(solution)/shard_map/cxzk,kw->cxzw/dot_general | solution.py:333
  (15 shorter events, 0.2 us)
Async XLA Ops:
  0.6 1.7 %copy-start.9 = (pred[384]{0:T(512)(128)(4,1)S(1)}, pred[384]{0:T(512)(128)(4,1)}, u32[]{:S(2)}) copy-start(pred[384]{0:T(512)(128)(4,1)} %constant.18.clone.1) | copy-start | bytes 1156
  0.6 2.5 %copy-start.6 = (bf16[3,4,4,1,1,1]{0,2,5,4,3,1:T(4,128)(2,1)S(1)}, bf16[3,4,4,1,1,1]{0,2,5,4,3,1:T(4,128)(2,1)}, u32[]{:S(2)}) copy-start(bf16[3,4,4,1,1,1]{0,2,5,4,3,1:T(4,128)(2,1)} %constant.42) | copy-start | bytes 292
  0.7 1.5 %copy-start = (bf16[4,1,128,640]{3,2,1,0:T(8,128)(2,1)S(1)}, bf16[4,1,128,640]{3,2,1,0:T(8,128)(2,1)}, u32[]{:S(2)}) copy-start(bf16[4,1,128,640]{3,2,1,0:T(8,128)(2,1)} %param.21) | copy-start | bytes 1966084
  0.7 2.5 %copy-start.3 = (bf16[3,3,32,3,32]{4,2,3,1,0:T(8,128)(2,1)S(1)}, bf16[3,3,32,3,32]{4,2,3,1,0:T(8,128)(2,1)}, u32[]{:S(2)}) copy-start(bf16[3,3,32,3,32]{4,2,3,1,0:T(8,128)(2,1)} %param.25) | copy-start | bytes 165892
  4.6 1.3 copy-start.7
  4.7 1.8 %copy-start.1 = (bf16[4,128,384]{2,1,0:T(8,128)(2,1)S(1)}, bf16[4,128,384]{2,1,0:T(8,128)(2,1)}, u32[]{:S(2)}) copy-start(bf16[4,128,384]{2,1,0:T(8,128)(2,1)} %slice_select_fusion) | copy-start | bytes 1179652
  6.6 2.0 %copy-start.8 = (bf16[3,3,32,3,2]{2,4,3,1,0:T(2,128)(2,1)S(1)}, bf16[3,3,32,3,2]{2,4,3,1,0:T(2,128)(2,1)}, u32[]{:S(2)}) copy-start(bf16[3,3,32,3,2]{2,4,3,1,0:T(2,128)(2,1)} %param.24) | copy-start | bytes 10372
  82.4 0.8 copy-start.4
  85.3 49.1 %all-to-all-start = ((bf16[4,1,128,640]{3,0,1,2:T(4,128)(2,1)}), bf16[4,1,128,640]{3,0,1,2:T(4,128)(2,1)S(1)}, u32[]{:S(2)}, u32[]{:S(2)}) async-start(bf16[4,1,128,640]{3,0,1,2:T(4,128)(2,1)} %copy.99), calls=%async_computation | async-start | bytes 1310720 | tf_op jit(solution)/shard_map/all_to_all | solution.py:785
  112.7 18.4 %copy-start.5 = (s32[32,320]{1,0:T(8,128)S(1)}, s32[32,320]{1,0:T(8,128)}, u32[]{:S(2)}) copy-start(s32[32,320]{1,0:T(8,128)} %param.22) | copy-start | bytes 122884
  132.1 2.4 %copy-start.2 = (bf16[4,4,32,640]{3,2,1,0:T(8,128)(2,1)S(1)}, bf16[4,4,32,640]{3,2,1,0:T(8,128)(2,1)}, u32[]{:S(2)}) copy-start(bf16[4,4,32,640]{3,2,1,0:T(8,128)(2,1)} %k_ref.1) | copy-start | bytes 1966084
  132.1 2.4 %copy-start.10 = (bf16[4,4,32,640]{3,2,1,0:T(8,128)(2,1)S(1)}, bf16[4,4,32,640]{3,2,1,0:T(8,128)(2,1)}, u32[]{:S(2)}) copy-start(bf16[4,4,32,640]{3,2,1,0:T(8,128)(2,1)} %param.19) | copy-start | bytes 1966084
  133.0 1.6 %copy-start.11 = (bf16[640,640,1,1]{1,0,3,2:T(8,128)(2,1)S(1)}, bf16[640,640,1,1]{1,0,3,2:T(8,128)(2,1)}, u32[]{:S(2)}) copy-start(bf16[640,640,1,1]{1,0,3,2:T(8,128)(2,1)} %constant.44) | copy-start | bytes 2457604

commit v2 on v1

--- a/solution.py
+++ b/solution.py
@@ -512,20 +512,18 @@
         start_moving(1)
         finish_spreading(0)
 
-        @pl.loop(0, z_count + 6)
+        @pl.loop(0, z_count + 4, unroll=2)
         def _(row):
-            fill_taps(taps_zero, row, pixels_of(image_ref[row + 1], half_len))
-
-        @pl.loop(0, z_count + 4)
-        def _(row):
-            pre = conv_row(taps_zero, first_ref, row)
+            narrow = narrow_taps(image_ref, row + 1, half_len).astype(jnp.bfloat16)
+            taps_zero[row] = narrow
+            pre = dot(narrow, first_ref[...])
             pre_first[row] = pre
             act = pre / (1.0 + jnp.exp(-pre))
             fill_taps(
                 taps_first, row, jnp.where(row_inside(row - 2, me, z_count, length), act, 0.0)
             )
 
-        @pl.loop(0, z_count + 2)
+        @pl.loop(0, z_count + 2, unroll=2)
         def _(row):
             pre = conv_row(taps_first, middle_ref, row)
             pre_middle[row] = pre
@@ -534,7 +532,7 @@
                 taps_middle, row, jnp.where(row_inside(row - 1, me, z_count, length), act, 0.0)
             )
 
-        @pl.loop(0, z_count)
+        @pl.loop(0, z_count, unroll=2)
         def _(row):
             planes[row] = conv_row(taps_middle, last_ref, row).T[: 2 * slab_count]
 
@@ -570,7 +568,8 @@
         out_shape=(
             shape,
             jax.ShapeDtypeStruct((count, 2 * z_count, half_len), jnp.bfloat16),
-            taps(6), taps(4), taps(2), full(4), full(2),
+            jax.ShapeDtypeStruct((z_count + 4, half_len, LANES), jnp.bfloat16),
+            taps(4), taps(2), full(4), full(2),
         ),
         in_specs=[whole] * 10,
         out_specs=(whole,) * 7,
@@ -609,9 +608,23 @@
     return jnp.transpose(jnp.flip(kernel, (0, 1)), (0, 1, 3, 2))
 
 
-def pixels_of(plane, y_count):
-    filler = jnp.zeros((LANES - plane.shape[0], plane.shape[1]), plane.dtype)
-    return jnp.concatenate([plane, filler], axis=0).T[:y_count]
+def narrow_weights(kernel):
+    flat = kernel.reshape(9 * kernel.shape[2], kernel.shape[3])
+    return jnp.pad(flat, ((0, LANES - flat.shape[0]), (0, 0)))
+
+
+def narrow_taps(planes_ref, row, y_count):
+    pieces = []
+    for shift_z in range(3):
+        plane = planes_ref[row + shift_z]
+        width = plane.shape[1]
+        position = lax.broadcasted_iota(jnp.int32, plane.shape, 1)
+        pieces.append(jnp.where(position == 0, 0.0, pltpu.roll(plane, 1, 1)))
+        pieces.append(plane)
+        pieces.append(jnp.where(position >= y_count - 1, 0.0, pltpu.roll(plane, width - 1, 1)))
+    used = 9 * planes_ref.shape[1]
+    pieces.append(jnp.zeros((LANES - used, planes_ref.shape[2]), jnp.float32))
+    return jnp.concatenate(pieces, axis=0).T[:y_count]
 
 
 def fill_taps(taps_ref, row, values):
@@ -645,38 +658,37 @@
 
     def kernel(
         adjoint_ref, zero_ref, first_ref, middle_ref, pre_first_ref, pre_middle_ref,
-        back_middle_ref, back_last_ref, rounded_ref, out_taps, grad_taps, sums, out_ref,
+        back_middle_ref, back_last_ref, rounded_ref, out_taps, grad_taps, sums, narrow_sums, out_ref,
     ):
         me = my_position()
 
-        @pl.loop(0, z_count + 4)
+        @pl.loop(0, z_count + 2, unroll=2)
         def _(row):
-            fill_taps(out_taps, row, -pixels_of(adjoint_ref[row + 2], y_count))
-
-        @pl.loop(0, z_count + 2)
-        def _(row):
-            grad = conv_row(out_taps, back_last_ref, row) * silu_grad(pre_middle_ref[row])
+            narrow = (-narrow_taps(adjoint_ref, row + 2, y_count)).astype(jnp.bfloat16)
+            out_taps[row] = narrow
+            grad = dot(narrow, back_last_ref[...]) * silu_grad(pre_middle_ref[row])
             fill_taps(
                 grad_taps, row, jnp.where(row_inside(row - 1, me, z_count, length), grad, 0.0)
             )
 
         sums[...] = jnp.zeros_like(sums)
-
-        def gather(which, grad, taps_ref, row):
-            for shift_z in range(3):
-                sums[which, shift_z] += lax.dot_general(
-                    grad,
-                    taps_ref[row + shift_z],
-                    (((0,), (0,)), ((), ())),
-                    preferred_element_type=jnp.float32,
-                )
-
-        @pl.loop(0, z_count)
+        narrow_sums[...] = jnp.zeros_like(narrow_sums)
+
+        def over_pixels(left, right):
+            return lax.dot_general(
+                left, right, (((0,), (0,)), ((), ())), preferred_element_type=jnp.float32
+            )
+
+        @pl.loop(0, z_count, unroll=2)
         def _(row):
             grad = conv_row(grad_taps, back_middle_ref, row) * silu_grad(pre_first_ref[row + 2])
-            gather(0, grad.astype(jnp.bfloat16), zero_ref, row + 2)
-            gather(1, grad_taps[row + 1, :, LANES : 2 * LANES], first_ref, row + 1)
-            gather(2, out_taps[row + 2, :, LANES : 2 * LANES], middle_ref, row)
+            narrow_sums[0] += over_pixels(zero_ref[row + 2], grad.astype(jnp.bfloat16))
+            narrow_sums[1] += over_pixels(
+                out_taps[row + 1], middle_ref[row + 1, :, LANES : 2 * LANES]
+            )
+            center = grad_taps[row + 1, :, LANES : 2 * LANES]
+            for shift_z in range(3):
+                sums[shift_z] += over_pixels(center, first_ref[row + 1 + shift_z])
 
         out_ref[...] = jnp.zeros_like(out_ref)
         group = lax.broadcasted_iota(jnp.int32, (channels, LANES), 1) // channels
@@ -684,7 +696,7 @@
             for shift_y in range(3):
                 tap = shift_z * 3 + shift_y
                 lanes = slice(shift_y * LANES, (shift_y + 1) * LANES)
-                square = sums[1, shift_z, :, lanes]
+                square = sums[shift_z, :, lanes]
                 folded = jnp.zeros((channels, LANES), jnp.float32)
                 for shift_x in range(3):
                     picked = jnp.zeros((channels, LANES), jnp.float32)
@@ -701,9 +713,9 @@
                     folded = jnp.where(group == shift_x, picked, folded)
                 out_ref[tap * channels : (tap + 1) * channels] = folded
                 base = 9 * channels + tap * few
-                out_ref[base : base + few] = sums[0, shift_z, :, lanes].T[:few]
+                out_ref[base : base + few] = narrow_sums[0, tap * few : (tap + 1) * few]
                 base = base + 9 * few
-                out_ref[base : base + few] = sums[2, shift_z, :few, lanes]
+                out_ref[base : base + few] = narrow_sums[1, (8 - tap) * few : (9 - tap) * few]
         rounded_ref[...] = out_ref[...].astype(jnp.bfloat16)
 
     whole = pl.BlockSpec(memory_space=pltpu.VMEM)
@@ -713,9 +725,10 @@
         in_specs=[whole] * 8,
         out_specs=whole,
         scratch_shapes=[
-            pltpu.VMEM((z_count + 4, y_count, 3 * LANES), jnp.bfloat16),
+            pltpu.VMEM((z_count + 2, y_count, LANES), jnp.bfloat16),
             pltpu.VMEM((z_count + 2, y_count, 3 * LANES), jnp.bfloat16),
-            pltpu.VMEM((3, 3, LANES, 3 * LANES), jnp.float32),
+            pltpu.VMEM((3, LANES, 3 * LANES), jnp.float32),
+            pltpu.VMEM((2, LANES, LANES), jnp.float32),
             pltpu.VMEM((slot_rows, LANES), jnp.float32),
         ],
         compiler_params=pltpu.CompilerParams(vmem_limit_bytes=56 * 2**20),
@@ -751,7 +764,8 @@
     z_count = length // count
     rim = 4
     lanes = slab_count * weight_middle.shape[2]
-    if coil_maps.shape[1] != 1 or length % count or z_count % 8 or lanes != LANES or half_len % 16:
+    fits = coil_maps.shape[1] == 1 and length % count == 0 and z_count % 8 == 0
+    if not fits or lanes != LANES or half_len % 16 or 18 * slab_count > LANES:
         return shards_small_chunks(
             kspace,
             measured,
@@ -772,7 +786,7 @@
         cotangent,
         coil_maps,
         (
-            tap_rows(banded(weight_first, x_count)),
+            narrow_weights(banded(weight_first, x_count)),
             tap_rows(kernel_middle),
             tap_rows(kernel_last),
         ),
@@ -800,7 +814,7 @@
     local = backward_layers(
         adjoint,
         *kept,
-        (tap_rows(back_taps(kernel_middle)), tap_rows(back_taps(kernel_last))),
+        (tap_rows(back_taps(kernel_middle)), narrow_weights(back_taps(kernel_last))),
         z_count,
         length,
         half_len,

time: 136 us -> 130 us (0.956)
  Pallas kernels: 109 us -> 103 us
    pallas_call x1, Pallas kernels: 21.4 us -> 13 us  [backward_layers(): pl.pallas_call(kernel, out_shape=jax.ShapeDtypeStruct((slot_rows, LANES),...]
    pallas_call x1, Pallas kernels: 71 us -> 73.4 us  [images(): pl.pallas_call(kernel, out_shape=(shape, jax.ShapeDtypeStruct((count, 2 *...]
    pad x3 -> x1, local copies, waits for them, and re-layouts: 2.31 us -> 0.78 us  [tap_rows(): return jnp.pad(kernel, edge).reshape(3, 3 * LANES, LANES)]
  transfers between devices with their start and end apart: 1 -> 1, of which waited for: 0 -> 0; matrix products, arithmetic and copies ran while one was open for 5% -> 5% of each run, Pallas kernels for 28% -> 23%
where the time goes in v2:
time: 130 us
  Pallas kernels  103 us (79%)
  local copies, waits for them, and re-layouts  15 us (12%)
  other arithmetic  3.82 us (3%)
  starting transfers between devices  3.66 us (3%)
  matrix products  2.86 us (2%)
  between operations  1.68 us (1%)
    pallas_call x1, Pallas kernels, images(): pl.pallas_call(kernel, out_shape=(shape, jax.ShapeDtypeStruct((count, 2 *...  73.4 us
    pallas_call x1, Pallas kernels, total_of(): pl.pallas_call(kernel, out_shape=jax.ShapeDtypeStruct(values.shape, value...  16.3 us
    pallas_call x1, Pallas kernels, backward_layers(): pl.pallas_call(kernel, out_shape=jax.ShapeDtypeStruct((slot_rows, LANES),...  13 us
    all_to_all x1, starting transfers between devices, shards(): lax.all_to_all(spectra.astype(jnp.bfloat16), 'slab', split_axis=2, concat...  3.66 us
    unnamed x29, local copies, waits for them, and re-layouts  3.57 us
  transfers between devices with their start and end apart: 1, of which 0 were waited for; matrix products, arithmetic and copies ran while one was open for 5% of the time, Pallas kernels for 23%

profile of v2, /device:TPU:0, one launch (start us, length us, event | category | flops | bytes accessed | tf_op | source)
XLA Modules:
  0.0 129.7 jit_solution(4773931014824233838)
XLA Ops:
  0.6 0.0 copy-start.9
  0.6 0.0 copy-start.6
  0.7 0.0 copy-start
  0.7 0.0 copy-start.3
  0.7 1.5 %copy.90 = bf16[4,1,128,640]{2,3,0,1:T(8,128)(2,1)S(1)} copy(bf16[4,1,128,640]{3,2,1,0:T(8,128)(2,1)} %param.21) | data formatting | bytes 1310720 | tf_op args[3]
  2.2 0.0 copy-done
  2.2 0.2 slice.139
  2.4 0.0 copy-done.9
  2.4 0.8 slice_select_fusion
  3.2 0.0 copy-done.6
  3.2 0.0 copy-done.3
  3.2 0.5 convolution_bitcast_fusion.1
  3.7 1.0 copy.94
  4.6 0.0 copy-start.7
  4.7 0.0 copy-start.1
  4.7 1.3 %reshape.299.middle_ref = bf16[3,384,128]{2,1,0:T(8,128)(2,1)} reshape(bf16[3,3,4,32,4,32]{5,4,3,2,1,0:T(4,128)(2,1)S(1)} %copy.94) | data formatting | bytes 589824 | tf_op jit(solution)/shard_map/reshape | solution.py:604
  6.0 0.0 copy-done.7
  6.0 0.1 convolution_bitcast_fusion.2
  6.2 0.1 reshape.300
  6.3 0.2 copy.138
  6.5 0.0 copy-done.1
  6.5 0.1 fusion.4
  6.6 0.0 copy-start.8
  6.6 1.1 pad.24.maps_ref
  7.7 0.8 pad.26.clone
  8.5 0.0 copy-done.8
  8.5 0.1 convolution_bitcast_fusion.3
  8.7 0.1 reshape_reshape.3
  8.8 0.6 pad.25.first_ref
  9.4 73.4 %shard_map.201 = (f32[16,8,384]{2,1,0:T(8,128)}, bf16[16,16,320]{2,1,0:T(8,128)(2,1)}, bf16[12,320,128]{2,1,0:T(8,128)(2,1)}, bf16[12,320,384]{2,1,0:T(8,128)(2,...) custom-call(bf16[4,4,32,640]{3,2,1,0:T(8,128)(2,1)} %k_ref.1, ...), custom_call_target="tpu_custom_call" | custom-call | tf_op jit(solution)/shard_map/pallas_call | solution.py:566
  82.8 1.0 reshape.302
  83.8 0.3 fusion.19
  84.1 0.2 copy.121
  84.3 0.2 copy.122
  84.5 0.1 convert_element_type.65
  84.6 0.0 copy-start.4
  84.6 0.2 fusion.8
  84.8 0.6 copy-done.4
  85.4 0.5 convolution_bitcast_fusion
  85.9 0.1 fusion.17
  86.0 0.1 fusion.3
  86.2 1.3 %copy.100 = bf16[4,1,128,640]{3,0,1,2:T(4,128)(2,1)} copy(bf16[4,1,128,640]{2,3,0,1:T(8,128)(2,1)S(1)} %fusion.3) | data formatting | bytes 1310720 | tf_op jit(solution)/shard_map/convert_element_type | solution.py:800
  87.5 3.7 %all-to-all-start = ((bf16[4,1,128,640]{3,0,1,2:T(4,128)(2,1)}), bf16[4,1,128,640]{3,0,1,2:T(4,128)(2,1)S(1)}, u32[]{:S(2)}, u32[]{:S(2)}) async-start(bf16[4,1,128,640]{3,0,1,2:T(4,128)(2,1)} %copy.100), calls=%async_computation | async-start | bytes 1310720 | tf_op jit(solution)/shard_map/all_to_all | solution.py:799
  91.2 0.6 reshape.303
  91.8 0.9 copy.103
  92.7 0.6 pad.27.back_last_ref
  93.3 13.0 %shard_map.202 = bf16[512,128]{1,0:T(8,128)(2,1)} custom-call(f32[16,8,384]{2,1,0:T(8,128)} %get-tuple-element.12.adjoint_ref, bf16[12,320,128]{2,1,0:T(8,128)(2,1)} %get-tuple-element.13.zero_ref, bf16[12,320,384]{2,1,0:T(8,128)(2,1)} %get-tuple-element.14.first_ref, bf16[10,320,384]{2,1,0:T(8,128)(2,1)} %get-tuple-element.15.middle_ref, ...), custom_call_target="tpu_custom_call" | custom-call | tf_op jit(solution)/shard_map/pallas_call | solution.py:722
  106.3 16.3 %shard_map.203 = bf16[16,32,128]{2,1,0:T(8,128)(2,1)} custom-call(bf16[16,32,128]{2,1,0:T(8,128)(2,1)} %bitcast.95), custom_call_target="tpu_custom_call" | custom-call | tf_op jit(solution)/shard_map/pallas_call | solution.py:301
  122.6 0.9 convert_element_type.72
  123.5 0.9 slice.157
  124.4 0.1 reshape.309
  124.6 0.1 fusion.20
  124.6 0.1 reshape.307
  125.4 0.3 reshape.308
  125.7 0.0 copy-start.2
  125.7 0.0 copy-start.10
  125.8 0.8 copy.152
  126.6 0.6 maximum_bitcast_fusion.1
  127.2 0.1 fusion.21
  127.3 0.6 maximum_bitcast_fusion
  127.9 0.1 maximum_multiply_fusion
  128.0 0.0 all-to-all-done
  128.0 0.1 copy.101
  128.1 1.6 %fusion.1 = bf16[4,4,32,640]{3,2,1,0:T(8,128)(2,1)} fusion(bf16[4,4,32,640]{3,2,1,0:T(8,128)(2,1)S(1)} %bitcast.94, bf16[640,640,1,1]{1,0,3,2:T(8,128)(2,1)S(1)} %copy-done.11, bf16[4,4,32,640]{3,2,1,0:T(8,128)(2,1)S(1)} %copy-done.2, bf16[4,4,32,640]{3,2,1,0:T(8,128)(2,1)S(1)} %copy-done.10, f32[32,640]{1,0:T(8,128)S(1)} %maximum_multiply_fusion), kind=kOutput, calls=%fused_computation.7 | convolution fusion | flops 421724160 | bytes 3522560 | tf_op jit(solution)/shard_map/cxzk,kw->cxzw/dot_general | solution.py:333
  (15 shorter events, 0.2 us)
Async XLA Ops:
  0.6 1.7 %copy-start.9 = (pred[384]{0:T(512)(128)(4,1)S(1)}, pred[384]{0:T(512)(128)(4,1)}, u32[]{:S(2)}) copy-start(pred[384]{0:T(512)(128)(4,1)} %constant.18.clone.1) | copy-start | bytes 1156
  0.6 2.5 %copy-start.6 = (bf16[3,4,4,1,1,1]{0,2,5,4,3,1:T(4,128)(2,1)S(1)}, bf16[3,4,4,1,1,1]{0,2,5,4,3,1:T(4,128)(2,1)}, u32[]{:S(2)}) copy-start(bf16[3,4,4,1,1,1]{0,2,5,4,3,1:T(4,128)(2,1)} %constant.42) | copy-start | bytes 292
  0.7 1.5 %copy-start = (bf16[4,1,128,640]{3,2,1,0:T(8,128)(2,1)S(1)}, bf16[4,1,128,640]{3,2,1,0:T(8,128)(2,1)}, u32[]{:S(2)}) copy-start(bf16[4,1,128,640]{3,2,1,0:T(8,128)(2,1)} %param.21) | copy-start | bytes 1966084
  0.7 2.5 %copy-start.3 = (bf16[3,3,32,3,32]{4,2,3,1,0:T(8,128)(2,1)S(1)}, bf16[3,3,32,3,32]{4,2,3,1,0:T(8,128)(2,1)}, u32[]{:S(2)}) copy-start(bf16[3,3,32,3,32]{4,2,3,1,0:T(8,128)(2,1)} %param.25) | copy-start | bytes 165892
  4.6 1.3 %copy-start.7 = (bf16[3,3,2,3,32]{4,2,3,1,0:T(2,128)(2,1)S(1)}, bf16[3,3,2,3,32]{4,2,3,1,0:T(2,128)(2,1)}, u32[]{:S(2)}) copy-start(bf16[3,3,2,3,32]{4,2,3,1,0:T(2,128)(2,1)} %param.26) | copy-start | bytes 10372
  4.7 1.8 %copy-start.1 = (bf16[4,128,384]{2,1,0:T(8,128)(2,1)S(1)}, bf16[4,128,384]{2,1,0:T(8,128)(2,1)}, u32[]{:S(2)}) copy-start(bf16[4,128,384]{2,1,0:T(8,128)(2,1)} %slice_select_fusion) | copy-start | bytes 1179652
  6.6 1.9 %copy-start.8 = (bf16[3,3,32,3,2]{2,4,3,1,0:T(2,128)(2,1)S(1)}, bf16[3,3,32,3,2]{2,4,3,1,0:T(2,128)(2,1)}, u32[]{:S(2)}) copy-start(bf16[3,3,32,3,2]{2,4,3,1,0:T(2,128)(2,1)} %param.24) | copy-start | bytes 10372
  84.6 0.8 copy-start.4
  87.5 40.5 %all-to-all-start = ((bf16[4,1,128,640]{3,0,1,2:T(4,128)(2,1)}), bf16[4,1,128,640]{3,0,1,2:T(4,128)(2,1)S(1)}, u32[]{:S(2)}, u32[]{:S(2)}) async-start(bf16[4,1,128,640]{3,0,1,2:T(4,128)(2,1)} %copy.100), calls=%async_computation | async-start | bytes 1310720 | tf_op jit(solution)/shard_map/all_to_all | solution.py:799
  106.3 18.5 %copy-start.5 = (s32[32,320]{1,0:T(8,128)S(1)}, s32[32,320]{1,0:T(8,128)}, u32[]{:S(2)}) copy-start(s32[32,320]{1,0:T(8,128)} %param.22) | copy-start | bytes 122884
  125.7 2.4 %copy-start.2 = (bf16[4,4,32,640]{3,2,1,0:T(8,128)(2,1)S(1)}, bf16[4,4,32,640]{3,2,1,0:T(8,128)(2,1)}, u32[]{:S(2)}) copy-start(bf16[4,4,32,640]{3,2,1,0:T(8,128)(2,1)} %k_ref.1) | copy-start | bytes 1966084
  125.7 2.4 %copy-start.10 = (bf16[4,4,32,640]{3,2,1,0:T(8,128)(2,1)S(1)}, bf16[4,4,32,640]{3,2,1,0:T(8,128)(2,1)}, u32[]{:S(2)}) copy-start(bf16[4,4,32,640]{3,2,1,0:T(8,128)(2,1)} %param.19) | copy-start | bytes 1966084
  126.6 1.6 %copy-start.11 = (bf16[640,640,1,1]{1,0,3,2:T(8,128)(2,1)S(1)}, bf16[640,640,1,1]{1,0,3,2:T(8,128)(2,1)}, u32[]{:S(2)}) copy-start(bf16[640,640,1,1]{1,0,3,2:T(8,128)(2,1)} %constant.44) | copy-start | bytes 2457604

commit v3 on v2

--- a/solution.py
+++ b/solution.py
@@ -468,6 +468,8 @@
         def start_spreading(which):
             for step in range(1, slab_count):
                 moving(which, step, sources[which], False).wait_recv()
+            if which == 0:
+                start_moving(1)
             for block in range(slab_count):
                 rows = moved[which, block].reshape(coil_count * slab_rows, width)
                 product = dot(rows, yh_ref[...]) + dot(rows, yl_ref[...])
@@ -509,7 +511,7 @@
 
         start_moving(0)
         start_spreading(0)
-        start_moving(1)
+        start_spreading(1)
         finish_spreading(0)
 
         @pl.loop(0, z_count + 4, unroll=2)
@@ -543,7 +545,6 @@
         for step in range(1, count):
             refining(step, True).start()
         refined_ref[me] = refined_slots[slab]
-        start_spreading(1)
         for step in range(1, count):
             refining(step, False).wait_recv()
         finish_spreading(1)

time: 130 us -> 129 us (level)
  Pallas kernels: 103 us -> 101 us
    pallas_call x1, Pallas kernels: 73.4 us -> 72 us  [images(): pl.pallas_call(kernel, out_shape=(shape, jax.ShapeDtypeStruct((count, 2 *...]
where the time goes in v3:
time: 129 us; the launch traced here: 128 us
  Pallas kernels  101 us (78%)
  local copies, waits for them, and re-layouts  15 us (12%)
  other arithmetic  3.82 us (3%)
  starting transfers between devices  3.66 us (3%)
  matrix products  2.86 us (2%)
  between operations  1.68 us (1%)
    pallas_call x1, Pallas kernels, images(): pl.pallas_call(kernel, out_shape=(shape, jax.ShapeDtypeStruct((count, 2 *...  72 us
    pallas_call x1, Pallas kernels, total_of(): pl.pallas_call(kernel, out_shape=jax.ShapeDtypeStruct(values.shape, value...  16.3 us
    pallas_call x1, Pallas kernels, backward_layers(): pl.pallas_call(kernel, out_shape=jax.ShapeDtypeStruct((slot_rows, LANES),...  13 us
    all_to_all x1, starting transfers between devices, shards(): lax.all_to_all(spectra.astype(jnp.bfloat16), 'slab', split_axis=2, concat...  3.66 us
    unnamed x29, local copies, waits for them, and re-layouts  3.57 us
  transfers between devices with their start and end apart: 1, of which 0 were waited for; matrix products, arithmetic and copies ran while one was open for 5% of the time, Pallas kernels for 23%

profile of v3, /device:TPU:0, one launch (start us, length us, event | category | flops | bytes accessed | tf_op | source)
XLA Modules:
  0.0 128.3 jit_solution(2588507046821483393)
XLA Ops:
  0.6 0.0 copy-start.9
  0.6 0.0 copy-start.6
  0.7 0.0 copy-start
  0.7 0.0 copy-start.3
  0.7 1.5 %copy.90 = bf16[4,1,128,640]{2,3,0,1:T(8,128)(2,1)S(1)} copy(bf16[4,1,128,640]{3,2,1,0:T(8,128)(2,1)} %param.21) | data formatting | bytes 1310720 | tf_op args[3]
  2.2 0.0 copy-done
  2.2 0.2 slice.139
  2.4 0.0 copy-done.9
  2.4 0.8 slice_select_fusion
  3.2 0.0 copy-done.3
  3.2 0.5 convolution_bitcast_fusion.1
  3.7 1.0 copy.94
  4.6 0.0 copy-start.7
  4.7 0.0 copy-start.1
  4.7 1.3 %reshape.299.middle_ref = bf16[3,384,128]{2,1,0:T(8,128)(2,1)} reshape(bf16[3,3,4,32,4,32]{5,4,3,2,1,0:T(4,128)(2,1)S(1)} %copy.94) | data formatting | bytes 589824 | tf_op jit(solution)/shard_map/reshape | solution.py:605
  6.0 0.1 convolution_bitcast_fusion.2
  6.2 0.1 reshape.300
  6.3 0.2 copy.138
  6.5 0.1 fusion.4
  6.6 0.0 copy-start.8
  6.6 1.1 pad.24.maps_ref
  7.7 0.8 pad.26.clone
  8.5 0.1 convolution_bitcast_fusion.3
  8.7 0.1 reshape_reshape.3
  8.8 0.6 pad.25.first_ref
  9.4 72.0 %shard_map.201 = (f32[16,8,384]{2,1,0:T(8,128)}, bf16[16,16,320]{2,1,0:T(8,128)(2,1)}, bf16[12,320,128]{2,1,0:T(8,128)(2,1)}, bf16[12,320,384]{2,1,0:T(8,128)(2,...) custom-call(bf16[4,4,32,640]{3,2,1,0:T(8,128)(2,1)} %k_ref.1, ...), custom_call_target="tpu_custom_call" | custom-call | tf_op jit(solution)/shard_map/pallas_call | solution.py:567
  81.4 1.0 reshape.302
  82.5 0.3 fusion.19
  82.7 0.2 copy.121
  82.9 0.2 copy.122
  83.1 0.1 convert_element_type.65
  83.2 0.0 copy-start.4
  83.2 0.2 fusion.8
  83.4 0.6 copy-done.4
  84.0 0.5 convolution_bitcast_fusion
  84.5 0.1 fusion.17
  84.6 0.1 fusion.3
  84.8 1.3 %copy.100 = bf16[4,1,128,640]{3,0,1,2:T(4,128)(2,1)} copy(bf16[4,1,128,640]{2,3,0,1:T(8,128)(2,1)S(1)} %fusion.3) | data formatting | bytes 1310720 | tf_op jit(solution)/shard_map/convert_element_type | solution.py:801
  86.1 3.7 %all-to-all-start = ((bf16[4,1,128,640]{3,0,1,2:T(4,128)(2,1)}), bf16[4,1,128,640]{3,0,1,2:T(4,128)(2,1)S(1)}, u32[]{:S(2)}, u32[]{:S(2)}) async-start(bf16[4,1,128,640]{3,0,1,2:T(4,128)(2,1)} %copy.100), calls=%async_computation | async-start | bytes 1310720 | tf_op jit(solution)/shard_map/all_to_all | solution.py:800
  89.8 0.6 reshape.303
  90.4 0.9 copy.103
  91.3 0.6 pad.27.back_last_ref
  91.9 13.0 %shard_map.202 = bf16[512,128]{1,0:T(8,128)(2,1)} custom-call(f32[16,8,384]{2,1,0:T(8,128)} %get-tuple-element.12.adjoint_ref, bf16[12,320,128]{2,1,0:T(8,128)(2,1)} %get-tuple-element.13.zero_ref, bf16[12,320,384]{2,1,0:T(8,128)(2,1)} %get-tuple-element.14.first_ref, bf16[10,320,384]{2,1,0:T(8,128)(2,1)} %get-tuple-element.15.middle_ref, ...), custom_call_target="tpu_custom_call" | custom-call | tf_op jit(solution)/shard_map/pallas_call | solution.py:723
  104.9 16.3 %shard_map.203 = bf16[16,32,128]{2,1,0:T(8,128)(2,1)} custom-call(bf16[16,32,128]{2,1,0:T(8,128)(2,1)} %bitcast.95), custom_call_target="tpu_custom_call" | custom-call | tf_op jit(solution)/shard_map/pallas_call | solution.py:301
  121.2 0.9 convert_element_type.72
  122.1 0.9 slice.157
  123.0 0.1 reshape.309
  123.2 0.1 fusion.20
  123.2 0.1 reshape.307
  123.4 0.0 copy-done.5
  124.0 0.3 reshape.308
  124.3 0.0 copy-start.2
  124.4 0.0 copy-start.10
  124.4 0.8 copy.152
  125.2 0.6 maximum_bitcast_fusion.1
  125.8 0.1 fusion.21
  125.9 0.6 maximum_bitcast_fusion
  126.5 0.1 maximum_multiply_fusion
  126.6 0.0 all-to-all-done
  126.6 0.1 copy.101
  126.7 0.0 copy-done.2
  126.7 0.0 copy-done.10
  126.7 0.0 copy-done.11
  126.7 1.6 %fusion.1 = bf16[4,4,32,640]{3,2,1,0:T(8,128)(2,1)} fusion(bf16[4,4,32,640]{3,2,1,0:T(8,128)(2,1)S(1)} %bitcast.94, bf16[640,640,1,1]{1,0,3,2:T(8,128)(2,1)S(1)} %copy-done.11, bf16[4,4,32,640]{3,2,1,0:T(8,128)(2,1)S(1)} %copy-done.2, bf16[4,4,32,640]{3,2,1,0:T(8,128)(2,1)S(1)} %copy-done.10, f32[32,640]{1,0:T(8,128)S(1)} %maximum_multiply_fusion), kind=kOutput, calls=%fused_computation.7 | convolution fusion | flops 421724160 | bytes 3522560 | tf_op jit(solution)/shard_map/cxzk,kw->cxzw/dot_general | solution.py:333
  (15 shorter events, 0.2 us)
Async XLA Ops:
  0.6 1.7 %copy-start.9 = (pred[384]{0:T(512)(128)(4,1)S(1)}, pred[384]{0:T(512)(128)(4,1)}, u32[]{:S(2)}) copy-start(pred[384]{0:T(512)(128)(4,1)} %constant.18.clone.1) | copy-start | bytes 1156
  0.6 2.5 %copy-start.6 = (bf16[3,4,4,1,1,1]{0,2,5,4,3,1:T(4,128)(2,1)S(1)}, bf16[3,4,4,1,1,1]{0,2,5,4,3,1:T(4,128)(2,1)}, u32[]{:S(2)}) copy-start(bf16[3,4,4,1,1,1]{0,2,5,4,3,1:T(4,128)(2,1)} %constant.42) | copy-start | bytes 292
  0.7 1.5 %copy-start = (bf16[4,1,128,640]{3,2,1,0:T(8,128)(2,1)S(1)}, bf16[4,1,128,640]{3,2,1,0:T(8,128)(2,1)}, u32[]{:S(2)}) copy-start(bf16[4,1,128,640]{3,2,1,0:T(8,128)(2,1)} %param.21) | copy-start | bytes 1966084
  0.7 2.5 %copy-start.3 = (bf16[3,3,32,3,32]{4,2,3,1,0:T(8,128)(2,1)S(1)}, bf16[3,3,32,3,32]{4,2,3,1,0:T(8,128)(2,1)}, u32[]{:S(2)}) copy-start(bf16[3,3,32,3,32]{4,2,3,1,0:T(8,128)(2,1)} %param.25) | copy-start | bytes 165892
  4.6 1.3 %copy-start.7 = (bf16[3,3,2,3,32]{4,2,3,1,0:T(2,128)(2,1)S(1)}, bf16[3,3,2,3,32]{4,2,3,1,0:T(2,128)(2,1)}, u32[]{:S(2)}) copy-start(bf16[3,3,2,3,32]{4,2,3,1,0:T(2,128)(2,1)} %param.26) | copy-start | bytes 10372
  4.7 1.8 %copy-start.1 = (bf16[4,128,384]{2,1,0:T(8,128)(2,1)S(1)}, bf16[4,128,384]{2,1,0:T(8,128)(2,1)}, u32[]{:S(2)}) copy-start(bf16[4,128,384]{2,1,0:T(8,128)(2,1)} %slice_select_fusion) | copy-start | bytes 1179652
  6.6 1.9 %copy-start.8 = (bf16[3,3,32,3,2]{2,4,3,1,0:T(2,128)(2,1)S(1)}, bf16[3,3,32,3,2]{2,4,3,1,0:T(2,128)(2,1)}, u32[]{:S(2)}) copy-start(bf16[3,3,32,3,2]{2,4,3,1,0:T(2,128)(2,1)} %param.24) | copy-start | bytes 10372
  83.2 0.8 copy-start.4
  86.1 40.5 %all-to-all-start = ((bf16[4,1,128,640]{3,0,1,2:T(4,128)(2,1)}), bf16[4,1,128,640]{3,0,1,2:T(4,128)(2,1)S(1)}, u32[]{:S(2)}, u32[]{:S(2)}) async-start(bf16[4,1,128,640]{3,0,1,2:T(4,128)(2,1)} %copy.100), calls=%async_computation | async-start | bytes 1310720 | tf_op jit(solution)/shard_map/all_to_all | solution.py:800
  104.9 18.5 %copy-start.5 = (s32[32,320]{1,0:T(8,128)S(1)}, s32[32,320]{1,0:T(8,128)}, u32[]{:S(2)}) copy-start(s32[32,320]{1,0:T(8,128)} %param.22) | copy-start | bytes 122884
  124.3 2.4 %copy-start.2 = (bf16[4,4,32,640]{3,2,1,0:T(8,128)(2,1)S(1)}, bf16[4,4,32,640]{3,2,1,0:T(8,128)(2,1)}, u32[]{:S(2)}) copy-start(bf16[4,4,32,640]{3,2,1,0:T(8,128)(2,1)} %k_ref.1) | copy-start | bytes 1966084
  124.4 2.4 %copy-start.10 = (bf16[4,4,32,640]{3,2,1,0:T(8,128)(2,1)S(1)}, bf16[4,4,32,640]{3,2,1,0:T(8,128)(2,1)}, u32[]{:S(2)}) copy-start(bf16[4,4,32,640]{3,2,1,0:T(8,128)(2,1)} %param.19) | copy-start | bytes 1966084
  125.2 1.6 %copy-start.11 = (bf16[640,640,1,1]{1,0,3,2:T(8,128)(2,1)S(1)}, bf16[640,640,1,1]{1,0,3,2:T(8,128)(2,1)}, u32[]{:S(2)}) copy-start(bf16[640,640,1,1]{1,0,3,2:T(8,128)(2,1)} %constant.44) | copy-start | bytes 2457604
